TPU v7x, 32 devices: a whole 2x2x4 slice. The times are simulated.
32 devices in a mesh: blk: 8 (over z, y), head: 4 (over x, core).
Axes of the slice: x: 2, y: 2, z: 4, core: 2. Of those that a mesh axis runs over, the one named last changes fastest.
Arguments:
- query_rows: bfloat16 [8192, 1024], P(('blk', 'head')), may hold values from -8 to 8
- key_rows: bfloat16 [8192, 1024], P(('blk', 'head')), may hold values from -8 to 8
- value_rows: bfloat16 [8192, 1024], P(('blk', 'head')), may hold values from -6 to 6
- out_grad: bfloat16 [8192, 1024], P(('blk', 'head')), may hold values from -6 to 6
- expander_device: int32 [64, 4], P('blk'), may hold values from 0 to 7, all different within a row; in each aligned block of 8 rows (0 to 7, 8 to 15, ...) at most 8 rows name the same one
- expander_block: int32 [64, 4], P('blk'), may hold values from 0 to 7
- local_offset: int32 [64, 11], P('blk'), may hold values from -4 to 4
- live_count: int32 [64], P('blk'), may hold values from 3 to 4
- drop_seed: int32 [16, 64, 16], P('head', 'blk'), may hold values from 0 to 1048575
Outputs:
- attended: bfloat16 [8192, 1024], P(('blk', 'head'))
- query_grad: bfloat16 [8192, 1024], P(('blk', 'head'))
- key_grad: bfloat16 [8192, 1024], P(('blk', 'head'))
- value_grad: bfloat16 [8192, 1024], P(('blk', 'head'))
Inputs may be any that keep to these rules, and one draw needn't show every extreme that they name: `expander_device`: each row names 4 different devices. Among the rows of one device (aligned blocks of 8 rows), no device is named by more than 8 rows, and in every draw some device is named exactly 8 times by one device's rows.
All inputs are finite; a program needn't handle non-finite values.
Results may differ from a plain program's by a relative error of at most 0.012.
Values may be sent and summed in bfloat16 or wider, within the bound.
A program may use at most 128 MiB of HBM per device.

v0:
```python
import jax
import jax.numpy as jnp
from jax import lax
from jax.sharding import PartitionSpec as P

BS = 128
QB_DEV = 8
L = 11
E = 4
W = 4


KEEP_LEVEL = 102
KEEP_GAIN = 1024.0 / 922.0
MASKED = -1e30


def padded(block, sides, width):
    for axis, dim in sides:
        count = lax.axis_size(axis)
        forward = [(i, i + 1) for i in range(count - 1)]
        forward.append((count - 1, 0))
        backward = [(target, source) for source, target in forward]
        low = lax.ppermute(
            lax.slice_in_dim(block, block.shape[dim] - width, None, axis=dim), axis, forward
        )
        high = lax.ppermute(lax.slice_in_dim(block, 0, width, axis=dim), axis, backward)
        block = jnp.concatenate([low, block, high], axis=dim)
    return block


def shifted(block, axis, distance):
    devices = range(lax.axis_size(axis))
    route = [((i - distance) % len(devices), i) for i in devices]
    return lax.ppermute(block, axis, route)


def logical_right(value, amount):
    return lax.shift_right_logical(value, jnp.full(value.shape, amount, jnp.int32))


def keep_weights(seed_row, block_size):
    row_index = jnp.arange(block_size, dtype=jnp.int32)[:, None, None]
    col_index = jnp.arange(block_size, dtype=jnp.int32)[None, None, :]
    offset = row_index * block_size + col_index
    hashed = seed_row[:, None, :, None] * 40503 + offset[None]
    hashed = hashed ^ logical_right(hashed, 15)
    hashed = hashed * 739982445
    hashed = hashed ^ logical_right(hashed, 12)
    hashed = hashed * 695872825
    hashed = hashed ^ logical_right(hashed, 15)
    keep_scale = jnp.where(hashed & 1023 >= KEEP_LEVEL, KEEP_GAIN, 0.0).astype(jnp.float32)
    return keep_scale.reshape(seed_row.shape[0], block_size, -1)


def on_device(
    query_rows,
    key_rows,
    value_rows,
    out_grad,
    expander_device,
    expander_block,
    local_offset,
    live_count,
    drop_seed,
):
    head_count = lax.axis_size("head")
    head_index = lax.axis_index("head")
    share_rows = query_rows.shape[0]
    local_width = query_rows.shape[1] // head_count
    local_heads = drop_seed.shape[0]
    head_size = local_width // local_heads
    score_scale = head_size ** (-0.5)
    slot_count = 1 + L + E
    gathered = (
        lax.all_gather(query_rows, "head", axis=0, tiled=True),
        lax.all_gather(key_rows, "head", axis=0, tiled=True),
        lax.all_gather(value_rows, "head", axis=0, tiled=True),
        lax.all_gather(out_grad, "head", axis=0, tiled=True),
    )
    first_col = head_index * local_width
    query_local, key_local, value_local, grad_local = [
        lax.dynamic_slice_in_dim(member, first_col, local_width, 1) for member in gathered
    ]
    peer_count = lax.axis_size("blk")
    capacity = min(QB_DEV, max(2, (2 * QB_DEV * E + peer_count - 1) // peer_count))
    flat_device = expander_device.reshape(-1)
    matches = (flat_device[:, None] == jnp.arange(peer_count, dtype=jnp.int32)[None, :]).astype(
        jnp.int32
    )
    before = jnp.cumsum(matches, axis=0) - matches
    slot_rank = jnp.sum(before * matches, axis=1)
    far_position = flat_device * capacity + slot_rank
    far_live = jnp.arange(E, dtype=jnp.int32)[None, :] < live_count[:, None]
    asked_block = jnp.where(far_live, expander_block, -1)
    wanted = (
        jnp.full((peer_count * capacity,), -1, jnp.int32)
        .at[far_position]
        .set(asked_block.reshape(-1))
    )
    wanted_here = lax.all_to_all(
        wanted.reshape(peer_count, capacity), "blk", split_axis=0, concat_axis=0, tiled=True
    )
    key_blocks = key_local.reshape(QB_DEV, BS, local_width)
    value_blocks = value_local.reshape(QB_DEV, BS, local_width)
    stacked = jnp.stack([key_blocks, value_blocks], axis=1)
    widened = padded(stacked, (("blk", 0),), W)
    wanted_flat = wanted_here.reshape(-1)
    chosen = jnp.clip(wanted_flat, 0, QB_DEV - 1)
    asked_mask = (wanted_flat >= 0)[:, None, None]
    zero_block = jnp.zeros((), jnp.bfloat16)
    reply_shape = (peer_count, capacity, BS, local_width)
    far_key, far_value = (
        lax.all_to_all(
            jnp.where(asked_mask, key_blocks[chosen], zero_block).reshape(reply_shape),
            "blk",
            split_axis=0,
            concat_axis=0,
            tiled=True,
        ),
        lax.all_to_all(
            jnp.where(asked_mask, value_blocks[chosen], zero_block).reshape(reply_shape),
            "blk",
            split_axis=0,
            concat_axis=0,
            tiled=True,
        ),
    )
    near_count = QB_DEV + 2 * W
    far_total_count = peer_count * capacity
    key_table = jnp.concatenate(
        [widened[:, 0], far_key.reshape(far_total_count, BS, local_width)], axis=0
    )
    value_table = jnp.concatenate(
        [widened[:, 1], far_value.reshape(far_total_count, BS, local_width)], axis=0
    )
    local_block = jnp.arange(QB_DEV, dtype=jnp.int32)[:, None]
    self_slot = local_block + W
    near_slot = local_block + W + local_offset
    far_slot = near_count + far_position.reshape(QB_DEV, E)
    table_rows = jnp.concatenate([self_slot, near_slot, far_slot], axis=1)
    slot_number = jnp.arange(slot_count, dtype=jnp.int32)[None, :]
    live_slots = (slot_number <= L) | (slot_number - 1 - L < live_count[:, None])
    seed_rows = jnp.transpose(drop_seed, (1, 0, 2))
    query_grid = query_local.reshape(QB_DEV, BS, local_heads, head_size)
    grad_grid = grad_local.reshape(QB_DEV, BS, local_heads, head_size)

    def block_step(running, inputs):
        near_total, far_key_total, far_value_total = running
        query_block, grad_block, slot_row, live_row, seed_row = inputs
        key_block = key_table[slot_row].reshape(slot_count * BS, local_heads, head_size)
        value_block = value_table[slot_row].reshape(slot_count * BS, local_heads, head_size)
        live_keys = jnp.repeat(live_row, BS)
        keep_scale = keep_weights(seed_row, BS)
        scores = (
            jnp.einsum("qhd,khd->hqk", query_block, key_block, preferred_element_type=jnp.float32)
            * score_scale
        )
        scores = jnp.where(live_keys[None, None, :], scores, MASKED)
        largest = jnp.max(scores, axis=-1, keepdims=True)
        expterm = jnp.exp(scores - largest)
        attention = expterm / jnp.sum(expterm, axis=-1, keepdims=True)
        dropped = (attention * keep_scale).astype(jnp.bfloat16)
        attended_full = jnp.einsum(
            "hqk,khd->qhd", dropped, value_block, preferred_element_type=jnp.float32
        )
        row_delta = jnp.einsum("qhd,qhd->hq", grad_block.astype(jnp.float32), attended_full)
        drop_grad = jnp.einsum(
            "qhd,khd->hqk", grad_block, value_block, preferred_element_type=jnp.float32
        )
        score_grad = (
            attention * (drop_grad * keep_scale - row_delta[:, :, None]) * score_scale
        ).astype(jnp.bfloat16)
        query_block_grad = jnp.einsum(
            "hqk,khd->qhd", score_grad, key_block, preferred_element_type=jnp.float32
        )
        key_part = jnp.einsum(
            "hqk,qhd->khd", score_grad, query_block, preferred_element_type=jnp.float32
        )
        value_part = jnp.einsum(
            "hqk,qhd->khd", dropped, grad_block, preferred_element_type=jnp.float32
        )
        key_part = key_part.reshape(slot_count, BS, local_width)
        value_part = value_part.reshape(slot_count, BS, local_width)
        near_rows = slot_row[: L + 1]
        near_total = near_total.at[near_rows, 0].add(key_part[: L + 1])
        near_total = near_total.at[near_rows, 1].add(value_part[: L + 1])
        far_rows = slot_row[L + 1 :] - near_count
        far_key_total = far_key_total.at[far_rows].set(key_part[L + 1 :].astype(jnp.bfloat16))
        far_value_total = far_value_total.at[far_rows].set(value_part[L + 1 :].astype(jnp.bfloat16))
        return (
            (near_total, far_key_total, far_value_total),
            (attended_full.astype(jnp.bfloat16), query_block_grad.astype(jnp.bfloat16)),
        )

    start_totals = (
        jnp.zeros((near_count, 2, BS, local_width), jnp.float32),
        jnp.zeros((far_total_count, BS, local_width), jnp.bfloat16),
        jnp.zeros((far_total_count, BS, local_width), jnp.bfloat16),
    )
    totals, outputs = lax.scan(
        block_step, start_totals, (query_grid, grad_grid, table_rows, live_slots, seed_rows)
    )
    near_total, far_key_total, far_value_total = totals
    back_key, back_value = (
        lax.all_to_all(
            far_key_total.reshape(reply_shape), "blk", split_axis=0, concat_axis=0, tiled=True
        ),
        lax.all_to_all(
            far_value_total.reshape(reply_shape), "blk", split_axis=0, concat_axis=0, tiled=True
        ),
    )
    owner_match = (
        jnp.arange(QB_DEV, dtype=jnp.int32)[:, None] == wanted_here.reshape(1, -1)
    ).astype(jnp.bfloat16)
    far_key_sum = jnp.dot(
        owner_match,
        back_key.reshape(far_total_count, BS * local_width),
        preferred_element_type=jnp.float32,
    )
    far_value_sum = jnp.dot(
        owner_match,
        back_value.reshape(far_total_count, BS * local_width),
        preferred_element_type=jnp.float32,
    )
    from_below = shifted(near_total[QB_DEV + W :].astype(jnp.bfloat16), "blk", 1).astype(
        jnp.float32
    )
    from_above = shifted(near_total[:W].astype(jnp.bfloat16), "blk", -1).astype(jnp.float32)
    own_total = near_total[W : W + QB_DEV]
    own_total = own_total.at[:W].add(from_below)
    own_total = own_total.at[QB_DEV - W :].add(from_above)
    block_rows = QB_DEV * BS
    key_grad = (own_total[:, 0].reshape(QB_DEV, BS * local_width) + far_key_sum).astype(
        jnp.bfloat16
    )
    value_grad = (own_total[:, 1].reshape(QB_DEV, BS * local_width) + far_value_sum).astype(
        jnp.bfloat16
    )
    results = (
        outputs[0].reshape(block_rows, local_width),
        outputs[1].reshape(block_rows, local_width),
        key_grad.reshape(block_rows, local_width),
        value_grad.reshape(block_rows, local_width),
    )
    full_results = (
        lax.all_gather(results[0], "head", axis=1, tiled=True),
        lax.all_gather(results[1], "head", axis=1, tiled=True),
        lax.all_gather(results[2], "head", axis=1, tiled=True),
        lax.all_gather(results[3], "head", axis=1, tiled=True),
    )
    first_row = head_index * share_rows
    return tuple(
        (lax.dynamic_slice_in_dim(member, first_row, share_rows, 0) for member in full_results)
    )


def solution(mesh):
    in_specs = (
        P(("blk", "head"), None),
        P(("blk", "head"), None),
        P(("blk", "head"), None),
        P(("blk", "head"), None),
        P("blk", None),
        P("blk", None),
        P("blk", None),
        P("blk"),
        P("head", "blk", None),
    )
    out_specs = (
        P(("blk", "head"), None),
        P(("blk", "head"), None),
        P(("blk", "head"), None),
        P(("blk", "head"), None),
    )
    return jax.shard_map(
        on_device, mesh=mesh, in_specs=in_specs, out_specs=out_specs, check_vma=False
    )
```

profile of v0, /device:TPU:0, one launch (start us, length us, event | category | flops | bytes accessed | tf_op | source)
XLA Modules:
  0.0 996.8 jit_solution(1551561600383467240)
XLA Ops:
  12.2 7.3 all-to-all-start
  19.5 6.4 all-to-all-done
  26.5 8.5 all-gather.13.cloned.1.call-done
  38.8 20.3 %all-gather.11.cloned.1.call-done = bf16[1024,1024]{1,0:T(8,128)(2,1)} async-done(((bf16[256,1024]{1,0:T(8,128)(2,1)}), bf16[1024,1024]{1,0:T(8,128)(2,1)}) %all-gather.11.cloned.1.call-update) | async-done | bytes 2097168 | tf_op jit(solution)/shard_map/all_gather | solution.py:77
  63.1 5.2 broadcast_select_fusion
  68.3 98.9 %all_to_all.29 = bf16[8,8,128,256]{3,2,1,0:T(8,128)(2,1)} all-to-all(bf16[8,8,128,256]{3,2,1,0:T(8,128)(2,1)S(1)} %get-tuple-element.370), channel_id=1, replica_groups=mesh['blk'=8,'head'=4] {'blk'}, dimensions={0} | all-to-all | bytes 8388608 | tf_op jit(solution)/shard_map/all_to_all | solution.py:121
  167.3 4.7 all-to-all-start.1
  179.4 18.0 %all-gather.9.cloned.1.call-done = bf16[1024,1024]{1,0:T(8,128)(2,1)} async-done(((bf16[256,1024]{1,0:T(8,128)(2,1)}), bf16[1024,1024]{1,0:T(8,128)(2,1)}) %all-gather.9.cloned.1.call-update) | async-done | bytes 2097168 | tf_op jit(solution)/shard_map/all_gather | solution.py:76
  197.4 24.0 %all-gather.15.cloned.1.call-done = bf16[1024,1024]{1,0:T(8,128)(2,1)} async-done(((bf16[256,1024]{1,0:T(8,128)(2,1)}), bf16[1024,1024]{1,0:T(8,128)(2,1)}) %all-gather.15.cloned.1.call-update) | async-done | bytes 2097168 | tf_op jit(solution)/shard_map/all_gather | solution.py:79
  225.9 29.2 %collective-permute-done = bf16[4,2,128,256]{3,2,0,1:T(8,128)(2,1)} collective-permute-done((bf16[4,2,128,256]{3,2,0,1:T(8,128)(2,1)}, bf16[4,2,128,256]{3,2,0,1:T(8,128)(2,1)}, u32[]{:S(2)}, u32[]{:S(2)}) %collective-permute-start) | collective-permute-done | bytes 524320 | tf_op jit(solution)/shard_map/ppermute | solution.py:24
  259.6 7.0 all-to-all-done.1
  266.6 5.0 pad_maximum_fusion
  279.1 435.4 %while.24 = (s32[]{:T(128)}, f32[16,2,128,256]{3,2,1,0:T(8,128)}, bf16[64,128,256]{2,1,0:T(8,128)(2,1)}, bf16[64,128,256]{2,1,0:T(8,128)(2,1)}, bf16[8,128,4,64]...) while((s32[]{:T(128)}, f32[16,2,128,256]{3,2,1,0:T(8,128)}, ...), condition=%wide.region_10.11_spmd, body=%wide.region_3.10_spmd.sunk | while | flops 845073280 | bytes 125162392 | solution.py:201
  374.9 4.6 scatter_fusion
  483.8 4.6 scatter_fusion
  592.8 4.6 scatter_fusion
  714.5 16.6 %all-to-all-start.4 = ((bf16[8,8,128,256]{3,2,1,0:T(8,128)(2,1)}), bf16[8,8,128,256]{3,2,1,0:T(8,128)(2,1)}, u32[]{:S(2)}, u32[]{:S(2)}) async-start(bf16[8,8,128,256]{3,2,1,0:T(8,128)(2,1)} %bitcast.240), calls=%async_computation.4 | async-start | bytes 8388608 | tf_op jit(solution)/shard_map/all_to_all | solution.py:209
  732.4 93.3 %all-to-all-done.4 = bf16[8,8,128,256]{3,2,1,0:T(8,128)(2,1)} async-done(((bf16[8,8,128,256]{3,2,1,0:T(8,128)(2,1)}), bf16[8,8,128,256]{3,2,1,0:T(8,128)(2,1)}, u32[]{:S(2)}, u32[]{:S(2)}) %all-to-all-start.4) | async-done | bytes 4194336 | tf_op jit(solution)/shard_map/all_to_all | solution.py:209
  825.6 4.7 all-to-all-start.3
  842.4 71.7 %collective-permute-done.2 = bf16[4,2,128,256]{3,2,1,0:T(8,128)(2,1)S(1)} collective-permute-done((bf16[4,2,128,256]{3,2,1,0:T(8,128)(2,1)S(1)}, bf16[4,2,128,256]{3,2,1,0:T(8,128)(2,1)S(1)}, u32[]{:S(2)}, u32[]{:S(2)}) %collective-permute-start.2) | collective-permute-done | bytes 524320 | tf_op jit(solution)/shard_map/ppermute | solution.py:35
  916.4 4.7 copy.84
  925.0 4.7 copy.82
  935.7 28.0 %all-gather.23.cloned.1.call-done = bf16[1024,1024]{1,0:T(8,128)(2,1)} async-done(((bf16[1024,256]{1,0:T(8,128)(2,1)}), bf16[1024,1024]{1,0:T(8,128)(2,1)}) %all-gather.23.cloned.1.call-update) | async-done | bytes 2097168 | tf_op jit(solution)/shard_map/all_gather | solution.py:250
  965.6 22.6 %all-gather.21.cloned.1.call-done = bf16[1024,1024]{1,0:T(8,128)(2,1)} async-done(((bf16[1024,256]{1,0:T(8,128)(2,1)}), bf16[1024,1024]{1,0:T(8,128)(2,1)}) %all-gather.21.cloned.1.call-update) | async-done | bytes 2097168 | tf_op jit(solution)/shard_map/all_gather | solution.py:249
  (548 shorter events, 486.1 us)
Async XLA Ops:
  7.2 27.8 %all-gather.13.cloned.1.call-start = ((), (), s32[]{:S(2)}) async-start(), calls=%async_computation.7 | async-start | bytes 2621440 | tf_op jit(solution)/shard_map/all_gather | solution.py:78
  7.9 51.2 %all-gather.11.cloned.1.call-start = ((), (), s32[]{:S(2)}) async-start(), calls=%async_computation.6 | async-start | bytes 2621440 | tf_op jit(solution)/shard_map/all_gather | solution.py:77
  12.2 13.7 %all-to-all-start = ((s32[8,1,8]{2,1,0:T(1,128)}), s32[8,1,8]{2,1,0:T(1,128)S(1)}, u32[]{:S(2)}, u32[]{:S(2)}) async-start(s32[8,1,8]{2,1,0:T(1,128)} %bitcast.28), calls=%async_computation | async-start | bytes 8192 | tf_op jit(solution)/shard_map/all_to_all | solution.py:101
  167.3 11.9 %copy-start.11 = (s32[4,8,16]{2,1,0:T(8,128)S(1)}, s32[4,8,16]{2,1,0:T(8,128)}, u32[]{:S(2)}) copy-start(s32[4,8,16]{2,1,0:T(8,128)} %param.23) | copy-start | bytes 6148
  167.3 12.0 %copy-start.13 = (s32[8]{0:T(128)S(1)}, s32[8]{0:T(128)}, u32[]{:S(2)}) copy-start(s32[8]{0:T(128)} %param.22) | copy-start | bytes 100
  167.3 99.3 %all-to-all-start.1 = ((bf16[8,8,128,256]{3,2,1,0:T(8,128)(2,1)}), bf16[8,8,128,256]{3,2,1,0:T(8,128)(2,1)}, u32[]{:S(2)}, u32[]{:S(2)}) async-start(bf16[8,8,128,256]{3,2,1,0:T(8,128)(2,1)} %get-tuple-element.371), calls=%async_computation.1 | async-start | bytes 8388608 | tf_op jit(solution)/shard_map/all_to_all | solution.py:114
  172.0 25.4 %all-gather.9.cloned.1.call-start = ((), (), s32[]{:S(2)}) async-start(), calls=%async_computation.5 | async-start | bytes 2621440 | tf_op jit(solution)/shard_map/all_gather | solution.py:76
  172.7 48.7 %all-gather.15.cloned.1.call-start = ((), (), s32[]{:S(2)}) async-start(), calls=%async_computation.8 | async-start | bytes 2621440 | tf_op jit(solution)/shard_map/all_gather | solution.py:79
  174.5 80.6 %collective-permute-start = (bf16[4,2,128,256]{3,2,0,1:T(8,128)(2,1)}, bf16[4,2,128,256]{3,2,0,1:T(8,128)(2,1)}, u32[]{:S(2)}, u32[]{:S(2)}) collective-permute-start(bf16[4,2,128,256]{3,2,0,1:T(8,128)(2,1)} %get-tuple-element.366), channel_id=1, source_target_pairs={{0,4},{4,8},{8,12},{12,16},{16,20},{20,24},{24,28},{28,0},{1,5},{5... | collective-permute-start | bytes 1572872 | tf_op jit(solution)/shard_map/ppermute | solution.py:24
  176.3 78.8 %collective-permute-start.1 = (bf16[4,2,128,256]{3,2,0,1:T(8,128)(2,1)}, bf16[4,2,128,256]{3,2,0,1:T(8,128)(2,1)}, u32[]{:S(2)}, u32[]{:S(2)}) collective-permute-start(bf16[4,2,128,256]{3,2,0,1:T(8,128)(2,1)} %get-tuple-element.367), channel_id=1, source_target_pairs={{4,0},{8,4},{12,8},{16,12},{20,16},{24,20},{28,24},{0,28},{5,1},{9... | collective-permute-start | bytes 1572872 | tf_op jit(solution)/shard_map/ppermute | solution.py:27
  225.9 30.9 %copy-start.6 = (bf16[8,8,128,256]{3,2,1,0:T(8,128)(2,1)S(1)}, bf16[8,8,128,256]{3,2,1,0:T(8,128)(2,1)}, u32[]{:S(2)}) copy-start(bf16[8,8,128,256]{3,2,1,0:T(8,128)(2,1)} %all_to_all.29) | copy-start | bytes 12582916
  285.6 11.1 %copy-start.2 = (bf16[2048,4,64]{0,2,1:T(8,128)(2,1)}, bf16[2048,4,64]{0,2,1:T(8,128)(2,1)S(1)}, u32[]{:S(2)}) copy-start(bf16[2048,4,64]{0,2,1:T(8,128)(2,1)S(1)} %reshape.595) | copy-start | bytes 3145732 | tf_op jit(solution)/shard_map/while
  503.5 11.1 %copy-start.2 = (bf16[2048,4,64]{0,2,1:T(8,128)(2,1)}, bf16[2048,4,64]{0,2,1:T(8,128)(2,1)S(1)}, u32[]{:S(2)}) copy-start(bf16[2048,4,64]{0,2,1:T(8,128)(2,1)S(1)} %reshape.595) | copy-start | bytes 3145732 | tf_op jit(solution)/shard_map/while
  612.5 11.1 %copy-start.2 = (bf16[2048,4,64]{0,2,1:T(8,128)(2,1)}, bf16[2048,4,64]{0,2,1:T(8,128)(2,1)S(1)}, u32[]{:S(2)}) copy-start(bf16[2048,4,64]{0,2,1:T(8,128)(2,1)S(1)} %reshape.595) | copy-start | bytes 3145732 | tf_op jit(solution)/shard_map/while
  666.7 11.1 %copy-start.2 = (bf16[2048,4,64]{0,2,1:T(8,128)(2,1)}, bf16[2048,4,64]{0,2,1:T(8,128)(2,1)S(1)}, u32[]{:S(2)}) copy-start(bf16[2048,4,64]{0,2,1:T(8,128)(2,1)S(1)} %reshape.595) | copy-start | bytes 3145732 | tf_op jit(solution)/shard_map/while
  714.5 16.6 %copy-start.7 = (bf16[8,128,4,64]{1,3,2,0:T(8,128)(2,1)S(1)}, bf16[8,128,4,64]{1,3,2,0:T(8,128)(2,1)}, u32[]{:S(2)}) copy-start(bf16[8,128,4,64]{1,3,2,0:T(8,128)(2,1)} %get-tuple-element.288) | copy-start | bytes 1572868
  714.5 111.1 %all-to-all-start.4 = ((bf16[8,8,128,256]{3,2,1,0:T(8,128)(2,1)}), bf16[8,8,128,256]{3,2,1,0:T(8,128)(2,1)}, u32[]{:S(2)}, u32[]{:S(2)}) async-start(bf16[8,8,128,256]{3,2,1,0:T(8,128)(2,1)} %bitcast.240), calls=%async_computation.4 | async-start | bytes 8388608 | tf_op jit(solution)/shard_map/all_to_all | solution.py:209
  731.1 200.4 %all-gather.19.cloned.1.call-start = ((), (), s32[]{:S(2)}) async-start(), calls=%async_computation.10 | async-start | bytes 2621440 | tf_op jit(solution)/shard_map/all_gather | solution.py:248
  825.6 99.3 %all-to-all-start.3 = ((bf16[8,8,128,256]{3,2,1,0:T(8,128)(2,1)}), bf16[8,8,128,256]{3,2,1,0:T(8,128)(2,1)}, u32[]{:S(2)}, u32[]{:S(2)}) async-start(bf16[8,8,128,256]{3,2,1,0:T(8,128)(2,1)} %bitcast.241), calls=%async_computation.3 | async-start | bytes 8388608 | tf_op jit(solution)/shard_map/all_to_all | solution.py:206
  830.4 103.2 %all-gather.17.cloned.1.call-start = ((), (), s32[]{:S(2)}) async-start(), calls=%async_computation.9 | async-start | bytes 2621440 | tf_op jit(solution)/shard_map/all_gather | solution.py:247
  831.7 132.0 %all-gather.23.cloned.1.call-start = ((), (), s32[]{:S(2)}) async-start(), calls=%async_computation.12 | async-start | bytes 2621440 | tf_op jit(solution)/shard_map/all_gather | solution.py:250
  834.3 79.8 %collective-permute-start.2 = (bf16[4,2,128,256]{3,2,1,0:T(8,128)(2,1)S(1)}, bf16[4,2,128,256]{3,2,1,0:T(8,128)(2,1)S(1)}, u32[]{:S(2)}, u32[]{:S(2)}) collective-permute-start(bf16[4,2,128,256]{3,2,1,0:T(8,128)(2,1)S(1)} %get-tuple-element.363), channel_id=1, source_target_pairs={{28,0},{0,4},{4,8},{8,12},{12,16},{16,20},{20,24},{24,28},{29,1},{... | collective-permute-start | bytes 1572872 | tf_op jit(solution)/shard_map/ppermute | solution.py:35
  836.2 79.2 %collective-permute-start.3 = (bf16[4,2,128,256]{3,2,1,0:T(8,128)(2,1)S(1)}, bf16[4,2,128,256]{3,2,1,0:T(8,128)(2,1)S(1)}, u32[]{:S(2)}, u32[]{:S(2)}) collective-permute-start(bf16[4,2,128,256]{3,2,1,0:T(8,128)(2,1)S(1)} %get-tuple-element.362), channel_id=1, source_target_pairs={{4,0},{8,4},{12,8},{16,12},{20,16},{24,20},{28,24},{0,28},{5,1},{9... | collective-permute-start | bytes 1572872 | tf_op jit(solution)/shard_map/ppermute | solution.py:35
  922.9 65.2 %all-gather.21.cloned.1.call-start = ((), (), s32[]{:S(2)}) async-start(), calls=%async_computation.11 | async-start | bytes 2621440 | tf_op jit(solution)/shard_map/all_gather | solution.py:249
  (48 other events, 216.2 us)
Sparse Core Ops, SparseCore 0:
  9.6 25.3 all-gather.12
  36.5 22.5 all-gather.10
  174.4 22.9 all-gather.8
  198.8 22.5 all-gather.14
  733.7 23.0 all-gather.18
  833.0 22.9 all-gather.16
  923.0 40.5 all-gather.22
  965.2 22.8 all-gather.20
where the time goes:
time: 1000 us; the launch traced here: 997 us
  waiting for transfers between devices  333 us (33%)
  local copies, waits for them, and re-layouts  271 us (27%)
  other arithmetic  121 us (12%)
  matrix products  113 us (11%)
  blocking collectives  98.9 us (10%)
  starting transfers between devices  43.1 us (4%)
  between operations  14.4 us (1%)
    all_to_all x1, blocking collectives, on_device(): lax.all_to_all(jnp.where(asked_mask, value_blocks[chosen], zero_block).re...  98.9 us
    all_to_all x1, waiting for transfers between devices, on_device(): lax.all_to_all(far_value_total.reshape(reply_shape), 'blk', split_axis=0,...  93.3 us
    ppermute x2, waiting for transfers between devices, shifted(): return lax.ppermute(block, axis, route)  71.7 us
    gather x16, local copies, waits for them, and re-layouts, block_step(): value_table[slot_row].reshape(slot_count * BS, local_heads, head_size)  42.2 us
    slice x24, local copies, waits for them, and re-layouts, block_step(): near_total = near_total.at[near_rows, 0].add(key_part[:L + 1])  36.8 us
    scatter-add x8, other arithmetic, block_step(): near_total = near_total.at[near_rows, 0].add(key_part[:L + 1])  36.4 us
    slice x24, local copies, waits for them, and re-layouts, block_step(): near_total = near_total.at[near_rows, 1].add(value_part[:L + 1])  35.7 us
    sub x8, matrix products, block_step(): expterm = jnp.exp(scores - largest)  34.6 us
  transfers between devices with their start and end apart: 16, of which 12 were waited for; matrix products, arithmetic and copies ran while one was open for 5% of the time, Pallas kernels for 0%

commit v1 on v0

v1 whole, which is shorter than its diff:
```python
import functools
import math

import jax
import jax.numpy as jnp
from jax import lax
from jax.experimental import pallas as pl
from jax.experimental.pallas import tpu as pltpu
from jax.sharding import PartitionSpec as P

BS = 128
QB_DEV = 8
L = 11
E = 4
W = 4
NB = 1 + L + E
DH = 64
PAIR = 2 * DH

KEEP_LEVEL = 102
KEEP_GAIN = 1024.0 / 922.0
MASKED = -1e30
LOG2E = math.log2(math.e)
CHUNK = 2 * BS
KEYS = NB * BS
FLUSH = 8


def logical_right(value, amount):
    return lax.shift_right_logical(value, jnp.full(value.shape, amount, jnp.int32))


def both_heads(rows):
    turned = rows.astype(jnp.float32).T
    upper = lax.broadcasted_iota(jnp.int32, turned.shape, 0) < DH
    return jnp.concatenate([jnp.where(upper, turned, 0.0), jnp.where(upper, 0.0, turned)], axis=1)


def one_each(wide):
    upper = lax.broadcasted_iota(jnp.int32, (PAIR, BS), 0) < DH
    return jnp.where(upper, wide[:, :BS], wide[:, BS:]).T


def dot(lhs, rhs, dims):
    return lax.dot_general(lhs, rhs, (dims, ((), ())), preferred_element_type=jnp.float32)


def attention_kernel(
    slots, live, q_ref, g_ref, kv_ref, word_ref, att_ref, dq_ref, grads_ref,
    acc, keys, values, scores, weights, kept, score_grad, stage, sems,
):
    c = pl.program_id(0)
    total_blocks = acc.shape[0]

    @pl.when(c == 0)
    def _():
        def clear(b, carry):
            acc[b] = jnp.zeros(acc.shape[1:], acc.dtype)
            return carry

        lax.fori_loop(0, total_blocks, clear, 0)

    for j in range(NB):
        keys[j * BS : (j + 1) * BS, :] = kv_ref[slots[c, j], :, :PAIR]
        values[j * BS : (j + 1) * BS, :] = kv_ref[slots[c, j], :, PAIR:]

    q_turned = (both_heads(q_ref[...]) * (DH**-0.5)).astype(jnp.bfloat16)
    g_wide = both_heads(g_ref[...])

    largest = jnp.full((8, 2 * BS), MASKED, jnp.float32)
    for at in range(0, KEYS, CHUNK):
        part = dot(keys[at : at + CHUNK, :], q_turned, ((1,), (0,)))
        if at + CHUNK > (1 + L) * BS:
            slot = at // BS + lax.broadcasted_iota(jnp.int32, part.shape, 0) // BS
            part = jnp.where(slot - (1 + L) < live[c], part, MASKED)
        scores[at : at + CHUNK, :] = part
        largest = jnp.maximum(largest, jnp.max(part.reshape(-1, 8, 2 * BS), axis=0))
    largest = jnp.max(largest, axis=0, keepdims=True)

    total = jnp.zeros((8, 2 * BS), jnp.float32)
    key_row = lax.broadcasted_iota(jnp.int32, (BS, 2 * BS), 0)
    for j in range(NB):
        rows = slice(j * BS, (j + 1) * BS)
        weight = jnp.exp2((scores[rows, :] - largest) * LOG2E)
        total = total + jnp.sum(weight.reshape(-1, 8, 2 * BS), axis=0)
        word = key_row + word_ref[0, j : j + 1, :]
        word = word ^ logical_right(word, 15)
        word = word * 739982445
        word = word ^ logical_right(word, 12)
        word = word * 695872825
        word = word ^ logical_right(word, 15)
        weights[rows, :] = weight.astype(jnp.bfloat16)
        kept[rows, :] = jnp.where((word & 1023) >= KEEP_LEVEL, weight, 0.0).astype(jnp.bfloat16)
    inverse = 1.0 / jnp.sum(total, axis=0, keepdims=True)

    out_turned = dot(values[...], kept[...], ((0,), (0,))) * (inverse * KEEP_GAIN)
    att_ref[...] = one_each(out_turned).astype(att_ref.dtype)
    delta = jnp.sum(out_turned * g_wide, axis=0, keepdims=True) * inverse
    g_turned = (g_wide * (inverse * KEEP_GAIN)).astype(jnp.bfloat16)

    for at in range(0, KEYS, CHUNK):
        rows = slice(at, at + CHUNK)
        drop_grad = dot(values[rows, :], g_turned, ((1,), (0,)))
        part = kept[rows, :]
        slope = (
            part.astype(jnp.float32) * drop_grad - weights[rows, :].astype(jnp.float32) * delta
        ).astype(jnp.bfloat16)
        score_grad[rows, :] = slope
        key_part = dot(slope, q_turned, ((1,), (1,)))
        value_part = dot(part, g_turned, ((1,), (1,)))
        for half in range(CHUNK // BS):
            here = slice(half * BS, (half + 1) * BS)
            block = slots[c, at // BS + half]
            acc[block, :, :PAIR] += key_part[here, :]
            acc[block, :, PAIR:] += value_part[here, :]
    q_grad = dot(keys[...], score_grad[...], ((0,), (0,))) * (DH**-0.5)
    dq_ref[...] = one_each(q_grad).astype(dq_ref.dtype)

    @pl.when(c == pl.num_programs(0) - 1)
    def _():
        copies = []
        for n in range(total_blocks // FLUSH):
            if n >= 2:
                copies[n - 2].wait()
            span = pl.ds(n * FLUSH, FLUSH)
            stage[n % 2] = acc[span].astype(stage.dtype)
            copy = pltpu.make_async_copy(stage.at[n % 2], grads_ref.at[span], sems.at[n % 2])
            copy.start()
            copies.append(copy)
        for copy in copies[-2:]:
            copy.wait()


def attend(slots, live, q, g, kv, words, pair):
    blocks = kv.shape[0]
    rows = q.shape[0]
    row_block = pl.BlockSpec((BS, PAIR), lambda c, s, n: (c, pair))
    out_block = pl.BlockSpec((BS, PAIR), lambda c, s, n: (c, 0))
    elements = rows * KEYS * 2
    return pl.pallas_call(
        attention_kernel,
        grid_spec=pltpu.PrefetchScalarGridSpec(
            num_scalar_prefetch=2,
            grid=(rows // BS,),
            in_specs=[
                row_block,
                row_block,
                pl.BlockSpec(
                    kv.shape, lambda c, s, n: (0, 0, 0), pipeline_mode=pl.Buffered(1)
                ),
                pl.BlockSpec((1, NB, 2 * BS), lambda c, s, n: (c, 0, 0)),
            ],
            out_specs=[out_block, out_block, pl.BlockSpec(memory_space=pl.ANY)],
            scratch_shapes=[
                pltpu.VMEM((blocks, BS, 2 * PAIR), jnp.float32),
                pltpu.VMEM((KEYS, PAIR), jnp.bfloat16),
                pltpu.VMEM((KEYS, PAIR), jnp.bfloat16),
                pltpu.VMEM((KEYS, 2 * BS), jnp.float32),
                pltpu.VMEM((KEYS, 2 * BS), jnp.bfloat16),
                pltpu.VMEM((KEYS, 2 * BS), jnp.bfloat16),
                pltpu.VMEM((KEYS, 2 * BS), jnp.bfloat16),
                pltpu.VMEM((2, FLUSH, BS, 2 * PAIR), jnp.bfloat16),
                pltpu.SemaphoreType.DMA((2,)),
            ],
        ),
        out_shape=[
            jax.ShapeDtypeStruct((rows, PAIR), jnp.bfloat16),
            jax.ShapeDtypeStruct((rows, PAIR), jnp.bfloat16),
            jax.ShapeDtypeStruct(kv.shape, jnp.bfloat16),
        ],
        compiler_params=pltpu.CompilerParams(
            dimension_semantics=("arbitrary",),
            vmem_limit_bytes=(24 << 20) + blocks * BS * 2 * PAIR * 6,
        ),
        cost_estimate=pl.CostEstimate(
            flops=elements * DH * 12 + elements * 400, bytes_accessed=16 << 20,
            transcendentals=elements,
        ),
    )(slots, live, q, g, kv, words)


def on_device(
    query_rows,
    key_rows,
    value_rows,
    out_grad,
    expander_device,
    expander_block,
    local_offset,
    live_count,
    drop_seed,
):
    head_count = lax.axis_size("head")
    share_rows = query_rows.shape[0]
    local_width = query_rows.shape[1] // head_count
    pairs = local_width // PAIR
    peer_count = lax.axis_size("blk")
    blocks = peer_count * QB_DEV
    block_rows = QB_DEV * BS

    def to_heads(members):
        sent = jnp.stack(
            [m.reshape(share_rows, head_count, local_width).transpose(1, 0, 2) for m in members],
            axis=1,
        )
        got = lax.all_to_all(sent, "head", split_axis=0, concat_axis=0, tiled=True)
        return [got[:, n].reshape(block_rows, local_width) for n in range(len(members))]

    def to_rows(members):
        sent = jnp.stack(
            [m.reshape(head_count, share_rows, m.shape[-1]) for m in members], axis=1
        )
        got = lax.all_to_all(sent, "head", split_axis=0, concat_axis=0, tiled=True)
        return [got[:, n] for n in range(len(members))]

    key_local, value_local, query_local, grad_local = to_heads(
        [key_rows, value_rows, query_rows, out_grad]
    )
    mine = lax.axis_index("blk") * QB_DEV + jnp.arange(QB_DEV, dtype=jnp.int32)[:, None]
    slots = jnp.concatenate(
        [mine, (mine + local_offset + blocks) % blocks, expander_device * QB_DEV + expander_block],
        axis=1,
    ).astype(jnp.int32)
    row = jnp.arange(BS, dtype=jnp.int32) * BS
    words = (drop_seed * 40503)[..., None] + row

    parts = []
    for pair in range(pairs):
        columns = slice(pair * PAIR, (pair + 1) * PAIR)
        kv = jnp.concatenate([key_local[:, columns], value_local[:, columns]], axis=1)
        kv = lax.all_gather(kv, "blk", axis=0, tiled=True).reshape(blocks, BS, 2 * PAIR)
        pair_words = jnp.concatenate([words[2 * pair], words[2 * pair + 1]], axis=-1)
        att, dq, grads = attend(slots, live_count, query_local, grad_local, kv, pair_words, pair)
        grads = lax.psum_scatter(
            grads.reshape(blocks * BS, 2 * PAIR), "blk", scatter_dimension=0, tiled=True
        )
        parts.append((att, dq, grads[:, :PAIR], grads[:, PAIR:]))
    locals_ = [jnp.concatenate([part[n] for part in parts], axis=1) for n in range(4)]
    out = to_rows(locals_)
    return tuple(m.transpose(1, 0, 2).reshape(share_rows, -1) for m in out)


def solution(mesh):
    rows = P(("blk", "head"), None)
    in_specs = (
        rows,
        rows,
        rows,
        rows,
        P("blk", None),
        P("blk", None),
        P("blk", None),
        P("blk"),
        P("head", "blk", None),
    )
    return jax.shard_map(
        on_device, mesh=mesh, in_specs=in_specs, out_specs=(rows,) * 4, check_vma=False
    )
```

time: 1000 us -> 419 us (0.42)
  local copies, waits for them, and re-layouts: 271 us -> 22.9 us
  other arithmetic: 121 us -> 4.08 us
  matrix products: 113 us -> 0 us
  waiting for transfers between devices: 333 us -> 247 us
  Pallas kernels: 0 us -> 73.2 us
  starting transfers between devices: 43.1 us -> 0.16 us
  blocking collectives: 98.9 us -> 58.2 us
    reduce_scatter x0 -> x2, waiting for transfers between devices: none -> 140 us  [on_device(): lax.psum_scatter(grads.reshape(blocks * BS, 2 * PAIR), 'blk', scatter_dim...]
    all_to_all x4 -> x0, waiting for transfers between devices: 108 us -> none  [the longest x1 93.3 us: on_device(): lax.all_to_all(far_value_total.reshape(reply_shape), 'blk', split_axis=0,...]
    ppermute x4 -> x0, waiting for transfers between devices: 101 us -> none  [the longest x2 71.7 us: shifted(): return lax.ppermute(block, axis, route)]
    gather x34 -> x0, local copies, waits for them, and re-layouts: 81.3 us -> none  [the longest x16 42.2 us: block_step(): value_table[slot_row].reshape(slot_count * BS, local_heads, head_size)]
    dot_general x42 -> x0, matrix products: 78.9 us -> none  [the longest x8 30.5 us: block_step(): jnp.einsum('qhd,khd->hqk', grad_block, value_block, preferred_element_typ...]
    pallas_call x0 -> x2, Pallas kernels: none -> 73.2 us  [attend(): pl.pallas_call(attention_kernel, grid_spec=pltpu.PrefetchScalarGridSpec(n...]
    slice x66 -> x5, local copies, waits for them, and re-layouts: 75.2 us -> 2.62 us  [the longest x2 2.13 us: on_device(): parts.append((att, dq, grads[:, :PAIR], grads[:, PAIR:]))]
    scatter-add x18 -> x0, other arithmetic: 70.2 us -> none  [the longest x8 36.4 us: block_step(): near_total = near_total.at[near_rows, 0].add(key_part[:L + 1])]
  transfers between devices with their start and end apart: 16 -> 4, of which waited for: 12 -> 4; matrix products, arithmetic and copies ran while one was open for 5% -> 1% of each run, Pallas kernels for 0% -> 17%
where the time goes in v1:
time: 419 us
  waiting for transfers between devices  247 us (59%)
  Pallas kernels  73.2 us (17%)
  blocking collectives  58.2 us (14%)
  local copies, waits for them, and re-layouts  22.9 us (5%)
  between operations  14 us (3%)
    reduce_scatter x2, waiting for transfers between devices, on_device(): lax.psum_scatter(grads.reshape(blocks * BS, 2 * PAIR), 'blk', scatter_dim...  140 us
    all_gather x2, waiting for transfers between devices, on_device(): lax.all_gather(kv, 'blk', axis=0, tiled=True).reshape(blocks, BS, 2 * PAIR)  107 us
    pallas_call x2, Pallas kernels, attend(): pl.pallas_call(attention_kernel, grid_spec=pltpu.PrefetchScalarGridSpec(n...  73.2 us
    all_to_all x1, blocking collectives, to_heads(): got = lax.all_to_all(sent, 'head', split_axis=0, concat_axis=0, tiled=True)  29.9 us
    all_to_all x1, blocking collectives, to_rows(): got = lax.all_to_all(sent, 'head', split_axis=0, concat_axis=0, tiled=True)  28.3 us
    unnamed x36, local copies, waits for them, and re-layouts  17.9 us
  transfers between devices with their start and end apart: 4, of which 4 were waited for; matrix products, arithmetic and copies ran while one was open for 1% of the time, Pallas kernels for 17%

profile of v1, /device:TPU:0, one launch (start us, length us, event | category | flops | bytes accessed | tf_op | source)
XLA Modules:
  0.0 419.0 jit_solution(6216561631702879418)
XLA Ops:
  7.2 1.3 copy.31
  8.6 1.2 copy.29
  9.8 1.0 copy.30
  10.8 1.0 copy.32
  11.8 1.5 pad_maximum_fusion
  13.3 2.4 copy.33
  15.6 29.9 %all_to_all.10 = bf16[4,4,256,256]{3,2,1,0:T(8,128)(2,1)S(1)} all-to-all(bf16[4,4,256,256]{3,2,1,0:T(8,128)(2,1)} %copy.33), channel_id=1, replica_groups=mesh['blk'=8,'head'=4] {'head'}, dimensions={0} | all-to-all | bytes 4194304 | tf_op jit(solution)/shard_map/all_to_all | solution.py:206
  48.4 73.2 %all-gather.3.cloned.1.call-done = bf16[8192,256]{1,0:T(8,128)(2,1)} async-done(((bf16[1024,256]{1,0:T(8,128)(2,1)}), bf16[8192,256]{1,0:T(8,128)(2,1)}) %all-gather.3.cloned.1.call-update) | async-done | bytes 4194320 | tf_op jit(solution)/shard_map/all_gather | solution.py:231
  121.5 2.2 copy-done.3
  123.7 36.6 %shard_map.120 = (bf16[1024,128]{1,0:T(8,128)(2,1)S(1)}, bf16[1024,128]{1,0:T(8,128)(2,1)S(1)}, bf16[64,128,256]{2,1,0:T(8,128)(2,1)S(1)}) custom-call(s32[8,16]{1,0:T(8,128)S(1)} %pad_add_fusion.2.slots, s32[8]{0:T(128)S(1)} %copy-done.4, bf16[1024,256]{1,0:T(8,128)(2,1)S(1)} %bitcast.68, bf16[1024,256]{1,0:T(8,128)(2,1)S(1)} %bitcast.66, ...), custom_call_target="tpu_custom_call" | custom-call | flops 4898947072 | bytes 16777216 | tf_op jit(solution)/shard_map/pallas_call | solution.py:140
  160.4 1.9 copy-done
  162.4 33.4 %all-gather.5.cloned.1.call-done = bf16[8192,256]{1,0:T(8,128)(2,1)} async-done(((bf16[1024,256]{1,0:T(8,128)(2,1)}), bf16[8192,256]{1,0:T(8,128)(2,1)}) %all-gather.5.cloned.1.call-update) | async-done | bytes 4194320 | tf_op jit(solution)/shard_map/all_gather | solution.py:231
  195.8 2.2 copy-done.2
  198.0 36.6 %shard_map.121 = (bf16[1024,128]{1,0:T(8,128)(2,1)S(1)}, bf16[1024,128]{1,0:T(8,128)(2,1)S(1)}, bf16[64,128,256]{2,1,0:T(8,128)(2,1)S(1)}) custom-call(s32[8,16]{1,0:T(8,128)S(1)} %pad_add_fusion.2.slots, s32[8]{0:T(128)S(1)} %copy-done.4, bf16[1024,256]{1,0:T(8,128)(2,1)S(1)} %bitcast.69, bf16[1024,256]{1,0:T(8,128)(2,1)S(1)} %bitcast.67, ...), custom_call_target="tpu_custom_call" | custom-call | flops 4898947072 | bytes 16777216 | tf_op jit(solution)/shard_map/pallas_call | solution.py:140
  234.6 2.0 copy-done.1
  236.8 49.1 %reduce-scatter.3.cloned.1.call-done = bf16[1024,256]{1,0:T(8,128)(2,1)} async-done(((bf16[8192,256]{1,0:T(8,128)(2,1)}), bf16[1024,256]{1,0:T(8,128)(2,1)}) %reduce-scatter.3.cloned.1.call-update) | async-done | bytes 524304 | tf_op jit(solution)/shard_map/reduce_scatter | solution.py:234
  286.0 1.1 fusion.3
  287.0 90.7 %reduce-scatter.5.cloned.1.call-done = bf16[1024,256]{1,0:T(8,128)(2,1)} async-done(((bf16[8192,256]{1,0:T(8,128)(2,1)}), bf16[1024,256]{1,0:T(8,128)(2,1)}) %reduce-scatter.5.cloned.1.call-update) | async-done | bytes 524304 | tf_op jit(solution)/shard_map/reduce_scatter | solution.py:234
  377.7 1.1 fusion.4
  379.2 28.3 %all_to_all.11 = bf16[4,4,256,256]{3,2,1,0:T(8,128)(2,1)S(1)} all-to-all(bf16[4,4,256,256]{3,2,1,0:T(8,128)(2,1)S(1)} %pad_maximum_fusion.1), channel_id=1, replica_groups=mesh['blk'=8,'head'=4] {'head'}, dimensions={0} | all-to-all | bytes 4194304 | tf_op jit(solution)/shard_map/all_to_all | solution.py:213
  407.9 1.0 copy.43
  409.1 1.0 copy.42
  410.3 1.0 copy.41
  411.5 1.0 copy.40
  (53 shorter events, 4.4 us)
Async XLA Ops:
  7.2 2.6 copy-start.5
  7.2 3.6 copy-start.6
  7.2 114.3 %all-gather.3.cloned.1.call-start = ((), (), s32[]{:S(2)}) async-start(), calls=%async_computation.4 | async-start | bytes 4718592 | tf_op jit(solution)/shard_map/all_gather | solution.py:231
  45.9 1.9 copy-start.9
  45.9 2.0 copy-start.10
  45.9 2.1 copy-start.8
  45.9 2.2 copy-start.7
  45.9 75.6 %copy-start.4 = (s32[8]{0:T(128)S(1)}, s32[8]{0:T(128)}, u32[]{:S(2)}) copy-start(s32[8]{0:T(128)} %live.3) | copy-start | bytes 100
  46.8 149.0 %all-gather.5.cloned.1.call-start = ((), (), s32[]{:S(2)}) async-start(), calls=%async_computation.5 | async-start | bytes 4718592 | tf_op jit(solution)/shard_map/all_gather | solution.py:231
  47.8 238.2 %reduce-scatter.3.cloned.1.call-start = ((), (), s32[]{:S(2)}) async-start(), calls=%async_computation.6 | async-start | bytes 4718592 | tf_op jit(solution)/shard_map/reduce_scatter | solution.py:234
  121.5 2.2 copy-start.3
  160.3 1.9 copy-start
  162.3 215.4 %reduce-scatter.5.cloned.1.call-start = ((), (), s32[]{:S(2)}) async-start(), calls=%async_computation.7 | async-start | bytes 4718592 | tf_op jit(solution)/shard_map/reduce_scatter | solution.py:234
  195.8 2.2 copy-start.2
  234.6 2.0 copy-start.1
Sparse Core Ops, SparseCore 0:
  46.9 74.5 all-gather.2
  124.2 71.5 all-gather.4
  199.4 86.4 reduce-scatter.2
  289.9 87.8 reduce-scatter.4

commit v2 on v1

--- a/solution.py
+++ b/solution.py
@@ -146,7 +146,7 @@
                 row_block,
                 row_block,
                 pl.BlockSpec(
-                    kv.shape, lambda c, s, n: (0, 0, 0), pipeline_mode=pl.Buffered(1)
+                    (blocks, BS, 2 * PAIR), lambda c, s, n: (0, 0, pair), pipeline_mode=pl.Buffered(1)
                 ),
                 pl.BlockSpec((1, NB, 2 * BS), lambda c, s, n: (c, 0, 0)),
             ],
@@ -166,7 +166,7 @@
         out_shape=[
             jax.ShapeDtypeStruct((rows, PAIR), jnp.bfloat16),
             jax.ShapeDtypeStruct((rows, PAIR), jnp.bfloat16),
-            jax.ShapeDtypeStruct(kv.shape, jnp.bfloat16),
+            jax.ShapeDtypeStruct((blocks, BS, 2 * PAIR), jnp.bfloat16),
         ],
         compiler_params=pltpu.CompilerParams(
             dimension_semantics=("arbitrary",),
@@ -177,6 +177,152 @@
             transcendentals=elements,
         ),
     )(slots, live, q, g, kv, words)
+
+
+MESH = pl.DeviceIdType.MESH
+
+
+def ring_place(n):
+    me = lax.axis_index("blk")
+    half = n // 2
+    z, y = me // 2, me % 2
+
+    def index_of(place):
+        place = (place + 2 * n) % n
+        back = place // half
+        return 2 * place * (1 - back) + (2 * (n - 1 - place) + 1) * back
+
+    return z * (1 - y) + (n - 1 - z) * y, index_of
+
+
+def meet(devices):
+    barrier = pltpu.get_barrier_semaphore()
+    for device in devices:
+        pl.semaphore_signal(barrier, inc=1, device_id={"blk": device}, device_id_type=MESH)
+    pl.semaphore_wait(barrier, len(devices))
+
+
+def gather_kernel(n, mine_ref, all_ref, own_sem, send_sem, recv_sem):
+    place, index_of = ring_place(n)
+    beside = (index_of(place + 1), index_of(place - 1))
+    meet(beside)
+    own = pltpu.make_async_copy(
+        mine_ref, all_ref.at[pl.ds(index_of(place) * QB_DEV, QB_DEV)], own_sem
+    )
+    own.start()
+    size = QB_DEV // 4
+
+    def copy_of(step, way, part):
+        origin = index_of(place - step if way == 0 else place + step)
+        first = (way * 2 + part) * size
+        there = all_ref.at[pl.ds(origin * QB_DEV + first, size)]
+        return pltpu.make_async_remote_copy(
+            src_ref=mine_ref.at[pl.ds(first, size)] if step == 0 else there,
+            dst_ref=there,
+            send_sem=send_sem.at[way, part, step],
+            recv_sem=recv_sem.at[way, part, step],
+            device_id={"blk": beside[way]},
+            device_id_type=MESH,
+        )
+
+    copies = {}
+    for step in range(n):
+        for part in range(2):
+            for way in range(2):
+                if step > 0:
+                    copies[step - 1, way, part].wait_recv()
+                if step < n - 1:
+                    copies[step, way, part] = copy_of(step, way, part)
+                    copies[step, way, part].start()
+    for copy in copies.values():
+        copy.wait_send()
+    own.wait()
+
+
+def gather_blocks(mine, n):
+    steps = pltpu.SemaphoreType.DMA((2, 2, n - 1))
+    return pl.pallas_call(
+        functools.partial(gather_kernel, n),
+        out_shape=jax.ShapeDtypeStruct((n * mine.shape[0],) + mine.shape[1:], mine.dtype),
+        in_specs=[pl.BlockSpec(memory_space=pl.ANY)],
+        out_specs=pl.BlockSpec(memory_space=pl.ANY),
+        scratch_shapes=[pltpu.SemaphoreType.DMA, steps, steps],
+        compiler_params=pltpu.CompilerParams(collective_id=0, has_side_effects=True),
+    )(mine)
+
+
+def reduce_kernel(n, pairs, *refs):
+    terms, sums = refs[:pairs], refs[pairs : 2 * pairs]
+    arrived, own, own_sem, send_sem, recv_sem = refs[2 * pairs :]
+    place, index_of = ring_place(n)
+    beside = (index_of(place + 1), index_of(place - 1))
+    meet(beside)
+    size = QB_DEV // 2
+    lanes = [(way, pair) for pair in range(pairs) for way in range(2)]
+
+    def term_of(step, way, pair):
+        owner = index_of(place - 1 - step if way == 0 else place + 1 + step)
+        return terms[pair].at[pl.ds(owner * QB_DEV + way * size, size)]
+
+    def fetch_of(step, way, pair):
+        slot = step % 2
+        return pltpu.make_async_copy(
+            term_of(step, way, pair), own.at[way, pair, slot], own_sem.at[way, pair, slot]
+        )
+
+    copies = {}
+    fetches = {}
+    for step in range(n):
+        for way, pair in lanes:
+            if step > 0:
+                copies[step - 1, way, pair].wait_recv()
+                fetches[step, way, pair].wait()
+                for b in range(size):
+                    got = arrived[way, pair, step - 1, b].astype(jnp.float32)
+                    got = (got + own[way, pair, step % 2, b].astype(jnp.float32)).astype(
+                        jnp.bfloat16
+                    )
+                    if step < n - 1:
+                        arrived[way, pair, step - 1, b] = got
+                    else:
+                        sums[pair][way * size + b] = got
+            if step < n - 1:
+                copies[step, way, pair] = pltpu.make_async_remote_copy(
+                    src_ref=term_of(0, way, pair) if step == 0 else arrived.at[way, pair, step - 1],
+                    dst_ref=arrived.at[way, pair, step],
+                    send_sem=send_sem.at[way, pair, step],
+                    recv_sem=recv_sem.at[way, pair, step],
+                    device_id={"blk": beside[way]},
+                    device_id_type=MESH,
+                )
+                copies[step, way, pair].start()
+                fetches[step + 1, way, pair] = fetch_of(step + 1, way, pair)
+                fetches[step + 1, way, pair].start()
+    for copy in copies.values():
+        copy.wait_send()
+
+
+def reduce_blocks(terms, n):
+    pairs = len(terms)
+    tail = terms[0].shape[1:]
+    chunk = (QB_DEV // 2,) + tail
+    steps = pltpu.SemaphoreType.DMA((2, pairs, n - 1))
+    return pl.pallas_call(
+        functools.partial(reduce_kernel, n, pairs),
+        out_shape=[jax.ShapeDtypeStruct((QB_DEV,) + tail, jnp.bfloat16)] * pairs,
+        in_specs=[pl.BlockSpec(memory_space=pl.ANY)] * pairs,
+        out_specs=[pl.BlockSpec(memory_space=pltpu.VMEM)] * pairs,
+        scratch_shapes=[
+            pltpu.VMEM((2, pairs, n - 1) + chunk, jnp.bfloat16),
+            pltpu.VMEM((2, pairs, 2) + chunk, jnp.bfloat16),
+            pltpu.SemaphoreType.DMA((2, pairs, 2)),
+            steps,
+            steps,
+        ],
+        compiler_params=pltpu.CompilerParams(
+            collective_id=1, has_side_effects=True, vmem_limit_bytes=(n + 12) << 20
+        ),
+    )(*terms)
 
 
 def on_device(
@@ -224,18 +370,22 @@
     row = jnp.arange(BS, dtype=jnp.int32) * BS
     words = (drop_seed * 40503)[..., None] + row
 
-    parts = []
+    mixed = []
     for pair in range(pairs):
         columns = slice(pair * PAIR, (pair + 1) * PAIR)
-        kv = jnp.concatenate([key_local[:, columns], value_local[:, columns]], axis=1)
-        kv = lax.all_gather(kv, "blk", axis=0, tiled=True).reshape(blocks, BS, 2 * PAIR)
+        mixed += [key_local[:, columns], value_local[:, columns]]
+    mixed = jnp.concatenate(mixed, axis=1).reshape(QB_DEV, BS, pairs * 2 * PAIR)
+    kv = gather_blocks(mixed, peer_count)
+    parts, terms = [], []
+    for pair in range(pairs):
         pair_words = jnp.concatenate([words[2 * pair], words[2 * pair + 1]], axis=-1)
         att, dq, grads = attend(slots, live_count, query_local, grad_local, kv, pair_words, pair)
-        grads = lax.psum_scatter(
-            grads.reshape(blocks * BS, 2 * PAIR), "blk", scatter_dimension=0, tiled=True
-        )
-        parts.append((att, dq, grads[:, :PAIR], grads[:, PAIR:]))
-    locals_ = [jnp.concatenate([part[n] for part in parts], axis=1) for n in range(4)]
+        parts.append((att, dq))
+        terms.append(grads)
+    sums = [m.reshape(block_rows, 2 * PAIR) for m in reduce_blocks(terms, peer_count)]
+    locals_ = [jnp.concatenate([part[n] for part in parts], axis=1) for n in range(2)]
+    locals_.append(jnp.concatenate([m[:, :PAIR] for m in sums], axis=1))
+    locals_.append(jnp.concatenate([m[:, PAIR:] for m in sums], axis=1))
     out = to_rows(locals_)
     return tuple(m.transpose(1, 0, 2).reshape(share_rows, -1) for m in out)
 

time: 419 us -> 318 us (0.76)
  waiting for transfers between devices: 247 us -> 25.2 us
  Pallas kernels: 73.2 us -> 239 us
  blocking collectives: 58.2 us -> 28.2 us
  between operations: 14 us -> 0.84 us
  local copies, waits for them, and re-layouts: 22.9 us -> 15.9 us
    pallas_call x0 -> x2, Pallas kernels: none -> 166 us  [the longest x1 83.7 us: gather_blocks(): pl.pallas_call(functools.partial(gather_kernel, n), out_shape=jax.ShapeDt...]
    reduce_scatter x2 -> x0, waiting for transfers between devices: 140 us -> none  [on_device(): lax.psum_scatter(grads.reshape(blocks * BS, 2 * PAIR), 'blk', scatter_dim...]
    all_gather x2 -> x0, waiting for transfers between devices: 107 us -> none  [on_device(): lax.all_gather(kv, 'blk', axis=0, tiled=True).reshape(blocks, BS, 2 * PAIR)]
    all_to_all x1 -> x0, blocking collectives: 29.9 us -> none  [to_heads(): got = lax.all_to_all(sent, 'head', split_axis=0, concat_axis=0, tiled=True)]
    all_to_all x0 -> x1, waiting for transfers between devices: none -> 25.2 us  [to_heads(): got = lax.all_to_all(sent, 'head', split_axis=0, concat_axis=0, tiled=True)]
    unnamed x36 -> x30, local copies, waits for them, and re-layouts: 17.9 us -> 13 us
    all_to_all x0 -> x1, starting transfers between devices: none -> 4.35 us  [to_heads(): got = lax.all_to_all(sent, 'head', split_axis=0, concat_axis=0, tiled=True)]
  transfers between devices with their start and end apart: 4 -> 1, of which waited for: 4 -> 1; matrix products, arithmetic and copies ran while one was open for 1% -> 0% of each run, Pallas kernels for 17% -> 0%
where the time goes in v2:
time: 318 us; the launch traced here: 317 us
  Pallas kernels  239 us (75%)
  blocking collectives  28.2 us (9%)
  waiting for transfers between devices  25.2 us (8%)
  local copies, waits for them, and re-layouts  15.9 us (5%)
  starting transfers between devices  4.35 us (1%)
  other arithmetic  3.51 us (1%)
    pallas_call x1, Pallas kernels, gather_blocks(): pl.pallas_call(functools.partial(gather_kernel, n), out_shape=jax.ShapeDt...  83.7 us
    pallas_call x1, Pallas kernels, reduce_blocks(): pl.pallas_call(functools.partial(reduce_kernel, n, pairs), out_shape=[jax...  81.8 us
    pallas_call x2, Pallas kernels, attend(): pl.pallas_call(attention_kernel, grid_spec=pltpu.PrefetchScalarGridSpec(n...  73.8 us
    all_to_all x1, blocking collectives, to_rows(): got = lax.all_to_all(sent, 'head', split_axis=0, concat_axis=0, tiled=True)  28.2 us
    all_to_all x1, waiting for transfers between devices, to_heads(): got = lax.all_to_all(sent, 'head', split_axis=0, concat_axis=0, tiled=True)  25.2 us
    unnamed x30, local copies, waits for them, and re-layouts  13 us
  transfers between devices with their start and end apart: 1, of which 1 were waited for; matrix products, arithmetic and copies ran while one was open for 0% of the time, Pallas kernels for 0%

profile of v2, /device:TPU:0, one launch (start us, length us, event | category | flops | bytes accessed | tf_op | source)
XLA Modules:
  0.0 317.2 jit_solution(13641452848060235214)
XLA Ops:
  0.7 1.3 copy.31
  2.0 1.2 copy.29
  3.2 1.0 copy.30
  4.2 1.0 copy.32
  5.2 1.5 pad_maximum_fusion
  6.7 2.4 copy.33
  9.1 4.4 %all-to-all-start = ((bf16[4,4,256,256]{3,2,1,0:T(8,128)(2,1)}), bf16[4,4,256,256]{3,2,1,0:T(8,128)(2,1)S(1)}, u32[]{:S(2)}, u32[]{:S(2)}) async-start(bf16[4,4,256,256]{3,2,1,0:T(8,128)(2,1)} %copy.33), calls=%async_computation | async-start | bytes 4194304 | tf_op jit(solution)/shard_map/all_to_all | solution.py:352
  14.0 25.2 %all-to-all-done = bf16[4,4,256,256]{3,2,1,0:T(8,128)(2,1)S(1)} async-done(((bf16[4,4,256,256]{3,2,1,0:T(8,128)(2,1)}), bf16[4,4,256,256]{3,2,1,0:T(8,128)(2,1)S(1)}, u32[]{:S(2)}, u32[]{:S(2)}) %all-to-all-start) | async-done | bytes 2097184 | tf_op jit(solution)/shard_map/all_to_all | solution.py:352
  39.5 1.2 pad_maximum_fusion.2
  40.7 83.7 %shard_map.120.kv_ref = bf16[64,128,512]{2,1,0:T(8,128)(2,1)} custom-call(bf16[8,128,512]{2,1,0:T(8,128)(2,1)} %bitcast.69), custom_call_target="tpu_custom_call" | custom-call | tf_op jit(solution)/shard_map/pallas_call | solution.py:244
  124.4 3.4 %copy-done = bf16[64,128,512]{2,1,0:T(8,128)(2,1)S(1)} copy-done((bf16[64,128,512]{2,1,0:T(8,128)(2,1)S(1)}, bf16[64,128,512]{2,1,0:T(8,128)(2,1)}, u32[]{:S(2)}) %copy-start) | copy-done | bytes 8388632
  127.8 36.9 %shard_map.122 = (bf16[1024,128]{1,0:T(8,128)(2,1)S(1)}, bf16[1024,128]{1,0:T(8,128)(2,1)S(1)}, bf16[64,128,256]{2,1,0:T(8,128)(2,1)S(1)}) custom-call(s32[8,16]{1,0:T(8,128)S(1)} %pad_add_fusion.2.slots, s32[8]{0:T(128)S(1)} %copy-done.1, bf16[1024,256]{1,0:T(8,128)(2,1)S(1)} %bitcast.67, bf16[1024,256]{1,0:T(8,128)(2,1)S(1)} %bitcast.65, ...), custom_call_target="tpu_custom_call" | custom-call | flops 4898947072 | bytes 16777216 | tf_op jit(solution)/shard_map/pallas_call | solution.py:140
  164.7 36.9 %shard_map.121 = (bf16[1024,128]{1,0:T(8,128)(2,1)S(1)}, bf16[1024,128]{1,0:T(8,128)(2,1)S(1)}, bf16[64,128,256]{2,1,0:T(8,128)(2,1)S(1)}) custom-call(s32[8,16]{1,0:T(8,128)S(1)} %pad_add_fusion.2.slots, s32[8]{0:T(128)S(1)} %copy-done.1, bf16[1024,256]{1,0:T(8,128)(2,1)S(1)} %bitcast.68, bf16[1024,256]{1,0:T(8,128)(2,1)S(1)} %bitcast.66, ...), custom_call_target="tpu_custom_call" | custom-call | flops 4898947072 | bytes 16777216 | tf_op jit(solution)/shard_map/pallas_call | solution.py:140
  201.5 81.8 %shard_map.123 = (bf16[8,128,256]{2,1,0:T(8,128)(2,1)S(1)}, bf16[8,128,256]{2,1,0:T(8,128)(2,1)S(1)}) custom-call(bf16[64,128,256]{2,1,0:T(8,128)(2,1)S(1)} %get-tuple-element.16.refs_0_, bf16[64,128,256]{2,1,0:T(8,128)(2,1)S(1)} %get-tuple-element.17.refs_1_), custom_call_target="tpu_custom_call" | custom-call | tf_op jit(solution)/shard_map/pallas_call | solution.py:310
  283.8 0.3 pad_maximum_fusion.1
  284.0 28.2 %all_to_all.10 = bf16[4,4,256,256]{3,2,1,0:T(8,128)(2,1)S(1)} all-to-all(bf16[4,4,256,256]{3,2,1,0:T(8,128)(2,1)S(1)} %pad_maximum_fusion.1), channel_id=1, replica_groups=mesh['blk'=8,'head'=4] {'head'}, dimensions={0} | all-to-all | bytes 4194304 | tf_op jit(solution)/shard_map/all_to_all | solution.py:359
  312.4 0.2 copy.47
  312.6 1.0 copy.43
  313.6 0.2 copy.46
  313.8 1.0 copy.42
  314.8 0.2 copy.45
  315.0 1.0 copy.41
  316.0 0.2 copy.44
  316.2 1.0 copy.40
  (36 shorter events, 1.4 us)
Async XLA Ops:
  0.6 2.6 copy-start.2
  0.6 3.6 %copy-start.3 = (bf16[256,1024]{1,0:T(8,128)(2,1)S(1)}, bf16[256,1024]{1,0:T(8,128)(2,1)}, u32[]{:S(2)}) copy-start(bf16[256,1024]{1,0:T(8,128)(2,1)} %param.12) | copy-start | bytes 1572868
  9.1 4.4 %copy-start.6 = (s32[8,4]{0,1:T(4,128)S(1)}, s32[8,4]{0,1:T(4,128)}, u32[]{:S(2)}) copy-start(s32[8,4]{0,1:T(4,128)} %param.13) | copy-start | bytes 388
  9.1 4.5 %copy-start.7 = (s32[8,4]{0,1:T(4,128)S(1)}, s32[8,4]{0,1:T(4,128)}, u32[]{:S(2)}) copy-start(s32[8,4]{0,1:T(4,128)} %param.14) | copy-start | bytes 388
  9.1 4.5 %copy-start.5 = (s32[8,11]{1,0:T(8,128)S(1)}, s32[8,11]{1,0:T(8,128)}, u32[]{:S(2)}) copy-start(s32[8,11]{1,0:T(8,128)} %param.15) | copy-start | bytes 1060
  9.1 4.7 %copy-start.4 = (s32[4,8,16]{2,1,0:T(8,128)S(1)}, s32[4,8,16]{2,1,0:T(8,128)}, u32[]{:S(2)}) copy-start(s32[4,8,16]{2,1,0:T(8,128)} %param.17) | copy-start | bytes 6148
  9.1 30.1 %all-to-all-start = ((bf16[4,4,256,256]{3,2,1,0:T(8,128)(2,1)}), bf16[4,4,256,256]{3,2,1,0:T(8,128)(2,1)S(1)}, u32[]{:S(2)}, u32[]{:S(2)}) async-start(bf16[4,4,256,256]{3,2,1,0:T(8,128)(2,1)} %copy.33), calls=%async_computation | async-start | bytes 4194304 | tf_op jit(solution)/shard_map/all_to_all | solution.py:352
  40.7 83.7 %copy-start.1 = (s32[8]{0:T(128)S(1)}, s32[8]{0:T(128)}, u32[]{:S(2)}) copy-start(s32[8]{0:T(128)} %live.3) | copy-start | bytes 100
  124.4 3.4 %copy-start = (bf16[64,128,512]{2,1,0:T(8,128)(2,1)S(1)}, bf16[64,128,512]{2,1,0:T(8,128)(2,1)}, u32[]{:S(2)}) copy-start(bf16[64,128,512]{2,1,0:T(8,128)(2,1)} %shard_map.120.kv_ref) | copy-start | bytes 25165828

commit v3 on v2

--- a/solution.py
+++ b/solution.py
@@ -195,17 +195,46 @@
     return z * (1 - y) + (n - 1 - z) * y, index_of
 
 
-def meet(devices):
+def meet(beside, heads):
     barrier = pltpu.get_barrier_semaphore()
+    devices = [{"blk": device} for device in beside]
+    devices += [{"head": (lax.axis_index("head") + k) % heads} for k in range(1, heads)]
     for device in devices:
-        pl.semaphore_signal(barrier, inc=1, device_id={"blk": device}, device_id_type=MESH)
+        pl.semaphore_signal(barrier, inc=1, device_id=device, device_id_type=MESH)
     pl.semaphore_wait(barrier, len(devices))
 
 
-def gather_kernel(n, mine_ref, all_ref, own_sem, send_sem, recv_sem):
+def exchange(heads, sent_ref, got_ref, own_sem, send_sem, recv_sem):
+    me = lax.axis_index("head")
+    started = [pltpu.make_async_copy(sent_ref.at[me], got_ref.at[me], own_sem)]
+    for k in range(1, heads):
+        peer = (me + k) % heads
+        started.append(
+            pltpu.make_async_remote_copy(
+                src_ref=sent_ref.at[peer],
+                dst_ref=got_ref.at[me],
+                send_sem=send_sem.at[k - 1],
+                recv_sem=recv_sem.at[k - 1],
+                device_id={"head": peer},
+                device_id_type=MESH,
+            )
+        )
+    for copy in started:
+        copy.start()
+    return started
+
+
+def exchange_semaphores(heads):
+    steps = pltpu.SemaphoreType.DMA((heads - 1,))
+    return [pltpu.SemaphoreType.DMA, steps, steps]
+
+
+def gather_kernel(
+    n, heads, mine_ref, sent_ref, all_ref, got_ref, own_sem, send_sem, recv_sem, *head_sems
+):
     place, index_of = ring_place(n)
     beside = (index_of(place + 1), index_of(place - 1))
-    meet(beside)
+    meet(beside, heads)
     own = pltpu.make_async_copy(
         mine_ref, all_ref.at[pl.ds(index_of(place) * QB_DEV, QB_DEV)], own_sem
     )
@@ -225,8 +254,11 @@
             device_id_type=MESH,
         )
 
+    swaps = []
     copies = {}
     for step in range(n):
+        if step == 1:
+            swaps = exchange(heads, sent_ref, got_ref, *head_sems)
         for part in range(2):
             for way in range(2):
                 if step > 0:
@@ -237,26 +269,32 @@
     for copy in copies.values():
         copy.wait_send()
     own.wait()
-
-
-def gather_blocks(mine, n):
+    for copy in swaps:
+        copy.wait()
+
+
+def gather_blocks(mine, sent, n):
     steps = pltpu.SemaphoreType.DMA((2, 2, n - 1))
     return pl.pallas_call(
-        functools.partial(gather_kernel, n),
-        out_shape=jax.ShapeDtypeStruct((n * mine.shape[0],) + mine.shape[1:], mine.dtype),
-        in_specs=[pl.BlockSpec(memory_space=pl.ANY)],
-        out_specs=pl.BlockSpec(memory_space=pl.ANY),
-        scratch_shapes=[pltpu.SemaphoreType.DMA, steps, steps],
+        functools.partial(gather_kernel, n, sent.shape[0]),
+        out_shape=[
+            jax.ShapeDtypeStruct((n * mine.shape[0],) + mine.shape[1:], mine.dtype),
+            jax.ShapeDtypeStruct(sent.shape, sent.dtype),
+        ],
+        in_specs=[pl.BlockSpec(memory_space=pl.ANY)] * 2,
+        out_specs=[pl.BlockSpec(memory_space=pl.ANY)] * 2,
+        scratch_shapes=[pltpu.SemaphoreType.DMA, steps, steps]
+        + exchange_semaphores(sent.shape[0]),
         compiler_params=pltpu.CompilerParams(collective_id=0, has_side_effects=True),
-    )(mine)
-
-
-def reduce_kernel(n, pairs, *refs):
-    terms, sums = refs[:pairs], refs[pairs : 2 * pairs]
-    arrived, own, own_sem, send_sem, recv_sem = refs[2 * pairs :]
+    )(mine, sent)
+
+
+def reduce_kernel(n, pairs, heads, sent_ref, *refs):
+    terms, got_ref, sums = refs[:pairs], refs[pairs], refs[pairs + 1 : 2 * pairs + 1]
+    arrived, own, own_sem, send_sem, recv_sem, *head_sems = refs[2 * pairs + 1 :]
     place, index_of = ring_place(n)
     beside = (index_of(place + 1), index_of(place - 1))
-    meet(beside)
+    meet(beside, heads)
     size = QB_DEV // 2
     lanes = [(way, pair) for pair in range(pairs) for way in range(2)]
 
@@ -270,9 +308,12 @@
             term_of(step, way, pair), own.at[way, pair, slot], own_sem.at[way, pair, slot]
         )
 
+    swaps = []
     copies = {}
     fetches = {}
     for step in range(n):
+        if step == 1:
+            swaps = exchange(heads, sent_ref, got_ref, *head_sems)
         for way, pair in lanes:
             if step > 0:
                 copies[step - 1, way, pair].wait_recv()
@@ -300,29 +341,34 @@
                 fetches[step + 1, way, pair].start()
     for copy in copies.values():
         copy.wait_send()
-
-
-def reduce_blocks(terms, n):
+    for copy in swaps:
+        copy.wait()
+
+
+def reduce_blocks(sent, terms, n):
     pairs = len(terms)
     tail = terms[0].shape[1:]
     chunk = (QB_DEV // 2,) + tail
     steps = pltpu.SemaphoreType.DMA((2, pairs, n - 1))
     return pl.pallas_call(
-        functools.partial(reduce_kernel, n, pairs),
-        out_shape=[jax.ShapeDtypeStruct((QB_DEV,) + tail, jnp.bfloat16)] * pairs,
-        in_specs=[pl.BlockSpec(memory_space=pl.ANY)] * pairs,
-        out_specs=[pl.BlockSpec(memory_space=pltpu.VMEM)] * pairs,
+        functools.partial(reduce_kernel, n, pairs, sent.shape[0]),
+        out_shape=[jax.ShapeDtypeStruct(sent.shape, sent.dtype)]
+        + [jax.ShapeDtypeStruct((QB_DEV,) + tail, jnp.bfloat16)] * pairs,
+        in_specs=[pl.BlockSpec(memory_space=pl.ANY)] * (pairs + 1),
+        out_specs=[pl.BlockSpec(memory_space=pl.ANY)]
+        + [pl.BlockSpec(memory_space=pltpu.VMEM)] * pairs,
         scratch_shapes=[
             pltpu.VMEM((2, pairs, n - 1) + chunk, jnp.bfloat16),
             pltpu.VMEM((2, pairs, 2) + chunk, jnp.bfloat16),
             pltpu.SemaphoreType.DMA((2, pairs, 2)),
             steps,
             steps,
-        ],
+        ]
+        + exchange_semaphores(sent.shape[0]),
         compiler_params=pltpu.CompilerParams(
             collective_id=1, has_side_effects=True, vmem_limit_bytes=(n + 12) << 20
         ),
-    )(*terms)
+    )(sent, *terms)
 
 
 def on_device(
@@ -344,24 +390,25 @@
     blocks = peer_count * QB_DEV
     block_rows = QB_DEV * BS
 
-    def to_heads(members):
-        sent = jnp.stack(
+    def for_heads(members):
+        return jnp.stack(
             [m.reshape(share_rows, head_count, local_width).transpose(1, 0, 2) for m in members],
             axis=1,
         )
-        got = lax.all_to_all(sent, "head", split_axis=0, concat_axis=0, tiled=True)
-        return [got[:, n].reshape(block_rows, local_width) for n in range(len(members))]
-
-    def to_rows(members):
-        sent = jnp.stack(
-            [m.reshape(head_count, share_rows, m.shape[-1]) for m in members], axis=1
-        )
-        got = lax.all_to_all(sent, "head", split_axis=0, concat_axis=0, tiled=True)
-        return [got[:, n] for n in range(len(members))]
-
-    key_local, value_local, query_local, grad_local = to_heads(
-        [key_rows, value_rows, query_rows, out_grad]
-    )
+
+    def for_rows(members):
+        return jnp.stack([m.reshape(head_count, share_rows, m.shape[-1]) for m in members], axis=1)
+
+    def swapped(sent):
+        return lax.all_to_all(sent, "head", split_axis=0, concat_axis=0, tiled=True)
+
+    def as_blocks(got):
+        return [got[:, n].reshape(block_rows, local_width) for n in range(got.shape[1])]
+
+    def as_rows(got):
+        return [got[:, n].transpose(1, 0, 2).reshape(share_rows, -1) for n in range(got.shape[1])]
+
+    key_local, value_local = as_blocks(swapped(for_heads([key_rows, value_rows])))
     mine = lax.axis_index("blk") * QB_DEV + jnp.arange(QB_DEV, dtype=jnp.int32)[:, None]
     slots = jnp.concatenate(
         [mine, (mine + local_offset + blocks) % blocks, expander_device * QB_DEV + expander_block],
@@ -375,19 +422,22 @@
         columns = slice(pair * PAIR, (pair + 1) * PAIR)
         mixed += [key_local[:, columns], value_local[:, columns]]
     mixed = jnp.concatenate(mixed, axis=1).reshape(QB_DEV, BS, pairs * 2 * PAIR)
-    kv = gather_blocks(mixed, peer_count)
+    kv, got = gather_blocks(mixed, for_heads([query_rows, out_grad]), peer_count)
+    query_local, grad_local = as_blocks(got)
     parts, terms = [], []
     for pair in range(pairs):
         pair_words = jnp.concatenate([words[2 * pair], words[2 * pair + 1]], axis=-1)
         att, dq, grads = attend(slots, live_count, query_local, grad_local, kv, pair_words, pair)
         parts.append((att, dq))
         terms.append(grads)
-    sums = [m.reshape(block_rows, 2 * PAIR) for m in reduce_blocks(terms, peer_count)]
-    locals_ = [jnp.concatenate([part[n] for part in parts], axis=1) for n in range(2)]
-    locals_.append(jnp.concatenate([m[:, :PAIR] for m in sums], axis=1))
-    locals_.append(jnp.concatenate([m[:, PAIR:] for m in sums], axis=1))
-    out = to_rows(locals_)
-    return tuple(m.transpose(1, 0, 2).reshape(share_rows, -1) for m in out)
+    row_results = [jnp.concatenate([part[n] for part in parts], axis=1) for n in range(2)]
+    got, *sums = reduce_blocks(for_rows(row_results), terms, peer_count)
+    sums = [m.reshape(block_rows, 2 * PAIR) for m in sums]
+    grads = [
+        jnp.concatenate([m[:, :PAIR] for m in sums], axis=1),
+        jnp.concatenate([m[:, PAIR:] for m in sums], axis=1),
+    ]
+    return tuple(as_rows(got) + as_rows(swapped(for_rows(grads))))
 
 
 def solution(mesh):

time: 318 us -> 293 us (0.921)
  blocking collectives: 28.2 us -> 0 us
  starting transfers between devices: 4.35 us -> 7.85 us
    all_to_all x1 -> x0, blocking collectives: 28.2 us -> none  [to_rows(): got = lax.all_to_all(sent, 'head', split_axis=0, concat_axis=0, tiled=True)]
    all_to_all x1 -> x2, starting transfers between devices: 4.35 us -> 7.85 us  [swapped(): return lax.all_to_all(sent, 'head', split_axis=0, concat_axis=0, tiled=True)]
    unnamed x30 -> x28, local copies, waits for them, and re-layouts: 13 us -> 10.9 us
    all_to_all x1 -> x2, waiting for transfers between devices: 25.2 us -> 23.8 us  [swapped(): return lax.all_to_all(sent, 'head', split_axis=0, concat_axis=0, tiled=True)]
  transfers between devices with their start and end apart: 1 -> 2, of which waited for: 1 -> 2; matrix products, arithmetic and copies ran while one was open for 0% -> 2% of each run, Pallas kernels for 0% -> 0%
where the time goes in v3:
time: 293 us; the launch traced here: 292 us
  Pallas kernels  241 us (82%)
  waiting for transfers between devices  23.8 us (8%)
  local copies, waits for them, and re-layouts  14.8 us (5%)
  starting transfers between devices  7.85 us (3%)
  other arithmetic  4.09 us (1%)
    pallas_call x1, Pallas kernels, gather_blocks(): pl.pallas_call(functools.partial(gather_kernel, n, sent.shape[0]), out_sh...  83.7 us
    pallas_call x1, Pallas kernels, reduce_blocks(): pl.pallas_call(functools.partial(reduce_kernel, n, pairs, sent.shape[0]),...  83.3 us
    pallas_call x2, Pallas kernels, attend(): pl.pallas_call(attention_kernel, grid_spec=pltpu.PrefetchScalarGridSpec(n...  73.7 us
    all_to_all x2, waiting for transfers between devices, swapped(): return lax.all_to_all(sent, 'head', split_axis=0, concat_axis=0, tiled=True)  23.8 us
    unnamed x28, local copies, waits for them, and re-layouts  10.9 us
    all_to_all x2, starting transfers between devices, swapped(): return lax.all_to_all(sent, 'head', split_axis=0, concat_axis=0, tiled=True)  7.85 us
  transfers between devices with their start and end apart: 2, of which 2 were waited for; matrix products, arithmetic and copies ran while one was open for 2% of the time, Pallas kernels for 0%

profile of v3, /device:TPU:0, one launch (start us, length us, event | category | flops | bytes accessed | tf_op | source)
XLA Modules:
  0.0 292.2 jit_solution(10204731813655065691)
XLA Ops:
  0.6 1.2 copy.45
  1.9 1.2 copy.46
  3.3 1.3 copy.47
  4.6 4.3 %all-to-all-start = ((bf16[4,2,256,256]{3,2,1,0:T(8,128)(2,1)}), bf16[4,2,256,256]{3,2,1,0:T(8,128)(2,1)S(1)}, u32[]{:S(2)}, u32[]{:S(2)}) async-start(bf16[4,2,256,256]{3,2,1,0:T(8,128)(2,1)} %copy.47), calls=%async_computation | async-start | bytes 2097152 | tf_op jit(solution)/shard_map/all_to_all | solution.py:403
  9.2 0.2 copy.48
  9.4 0.2 copy.49
  9.6 0.2 copy.50
  9.8 0.2 copy.51
  10.4 1.1 pad_maximum_fusion.2.sent_ref
  11.5 11.9 %all-to-all-done = bf16[4,2,256,256]{3,2,1,0:T(8,128)(2,1)S(1)} async-done(((bf16[4,2,256,256]{3,2,1,0:T(8,128)(2,1)}), bf16[4,2,256,256]{3,2,1,0:T(8,128)(2,1)S(1)}, u32[]{:S(2)}, u32[]{:S(2)}) %all-to-all-start) | async-done | bytes 1048608 | tf_op jit(solution)/shard_map/all_to_all | solution.py:403
  23.7 1.1 pad_maximum_fusion.1
  24.8 83.7 %shard_map.120 = (bf16[64,128,512]{2,1,0:T(8,128)(2,1)}, bf16[4,2,256,256]{3,2,1,0:T(8,128)(2,1)}) custom-call(bf16[8,128,512]{2,1,0:T(8,128)(2,1)} %bitcast.63, bf16[4,2,256,256]{3,2,1,0:T(8,128)(2,1)} %pad_maximum_fusion.2.sent_ref), custom_call_target="tpu_custom_call" | custom-call | tf_op jit(solution)/shard_map/pallas_call | solution.py:278
  108.5 1.3 fusion.2
  109.8 3.4 %copy-done = bf16[64,128,512]{2,1,0:T(8,128)(2,1)S(1)} copy-done((bf16[64,128,512]{2,1,0:T(8,128)(2,1)S(1)}, bf16[64,128,512]{2,1,0:T(8,128)(2,1)}, u32[]{:S(2)}) %copy-start) | copy-done | bytes 8388632
  113.1 36.9 %shard_map.122 = (bf16[1024,128]{1,0:T(8,128)(2,1)S(1)}, bf16[1024,128]{1,0:T(8,128)(2,1)S(1)}, bf16[64,128,256]{2,1,0:T(8,128)(2,1)S(1)}) custom-call(s32[8,16]{1,0:T(8,128)S(1)} %pad_add_fusion.2.slots, s32[8]{0:T(128)S(1)} %copy-done.1, bf16[1024,256]{1,0:T(8,128)(2,1)S(1)} %bitcast.61, bf16[1024,256]{1,0:T(8,128)(2,1)S(1)} %bitcast.59, ...), custom_call_target="tpu_custom_call" | custom-call | flops 4898947072 | bytes 16777216 | tf_op jit(solution)/shard_map/pallas_call | solution.py:140
  150.0 36.9 %shard_map.121 = (bf16[1024,128]{1,0:T(8,128)(2,1)S(1)}, bf16[1024,128]{1,0:T(8,128)(2,1)S(1)}, bf16[64,128,256]{2,1,0:T(8,128)(2,1)S(1)}) custom-call(s32[8,16]{1,0:T(8,128)S(1)} %pad_add_fusion.2.slots, s32[8]{0:T(128)S(1)} %copy-done.1, bf16[1024,256]{1,0:T(8,128)(2,1)S(1)} %bitcast.62, bf16[1024,256]{1,0:T(8,128)(2,1)S(1)} %bitcast.60, ...), custom_call_target="tpu_custom_call" | custom-call | flops 4898947072 | bytes 16777216 | tf_op jit(solution)/shard_map/pallas_call | solution.py:140
  187.1 83.3 %shard_map.123 = (bf16[4,2,256,256]{3,2,1,0:T(8,128)(2,1)S(1)}, bf16[8,128,256]{2,1,0:T(8,128)(2,1)S(1)}, bf16[8,128,256]{2,1,0:T(8,128)(2,1)S(1)}) custom-call(bf16[4,2,256,256]{3,2,1,0:T(8,128)(2,1)S(1)} %pad_maximum_fusion.3.sent_ref, bf16[64,128,256]{2,1,0:T(8,128)(2,1)S(1)} %get-tuple-element.21.refs_0_, bf16[64,128,256]{2,1,0:T(8,128)(2,1)S(1)} %get-tuple-element.22.refs_1_), custom_call_target="tpu_custom_call" | custom-call | tf_op jit(solution)/shard_map/pallas_call | solution.py:353
  270.7 1.1 pad_maximum_fusion.4
  271.7 3.5 %all-to-all-start.1 = ((bf16[4,2,256,256]{3,2,1,0:T(8,128)(2,1)}), bf16[4,2,256,256]{3,2,1,0:T(8,128)(2,1)S(1)}, u32[]{:S(2)}, u32[]{:S(2)}) async-start(bf16[4,2,256,256]{3,2,1,0:T(8,128)(2,1)} %pad_maximum_fusion.4), calls=%async_computation.1 | async-start | bytes 2097152 | tf_op jit(solution)/shard_map/all_to_all | solution.py:403
  275.5 1.0 copy.57
  276.8 1.0 copy.56
  277.8 11.9 %all-to-all-done.1 = bf16[4,2,256,256]{3,2,1,0:T(8,128)(2,1)S(1)} async-done(((bf16[4,2,256,256]{3,2,1,0:T(8,128)(2,1)}), bf16[4,2,256,256]{3,2,1,0:T(8,128)(2,1)S(1)}, u32[]{:S(2)}, u32[]{:S(2)}) %all-to-all-start.1) | async-done | bytes 1048608 | tf_op jit(solution)/shard_map/all_to_all | solution.py:403
  290.0 1.0 copy.59
  291.2 1.0 copy.58
  (43 shorter events, 2.3 us)
Async XLA Ops:
  3.2 5.7 %copy-start.6 = (s32[8,4]{0,1:T(4,128)S(1)}, s32[8,4]{0,1:T(4,128)}, u32[]{:S(2)}) copy-start(s32[8,4]{0,1:T(4,128)} %param.13) | copy-start | bytes 388
  3.2 5.8 %copy-start.7 = (s32[8,4]{0,1:T(4,128)S(1)}, s32[8,4]{0,1:T(4,128)}, u32[]{:S(2)}) copy-start(s32[8,4]{0,1:T(4,128)} %param.14) | copy-start | bytes 388
  3.3 5.9 %copy-start.4 = (s32[4,8,16]{2,1,0:T(8,128)S(1)}, s32[4,8,16]{2,1,0:T(8,128)}, u32[]{:S(2)}) copy-start(s32[4,8,16]{2,1,0:T(8,128)} %param.17) | copy-start | bytes 6148
  3.3 5.9 %copy-start.2 = (bf16[256,1024]{1,0:T(8,128)(2,1)S(1)}, bf16[256,1024]{1,0:T(8,128)(2,1)}, u32[]{:S(2)}) copy-start(bf16[256,1024]{1,0:T(8,128)(2,1)} %param.9) | copy-start | bytes 1572868
  4.6 5.0 %copy-start.3 = (bf16[256,1024]{1,0:T(8,128)(2,1)S(1)}, bf16[256,1024]{1,0:T(8,128)(2,1)}, u32[]{:S(2)}) copy-start(bf16[256,1024]{1,0:T(8,128)(2,1)} %param.12) | copy-start | bytes 1572868
  4.6 18.8 %all-to-all-start = ((bf16[4,2,256,256]{3,2,1,0:T(8,128)(2,1)}), bf16[4,2,256,256]{3,2,1,0:T(8,128)(2,1)S(1)}, u32[]{:S(2)}, u32[]{:S(2)}) async-start(bf16[4,2,256,256]{3,2,1,0:T(8,128)(2,1)} %copy.47), calls=%async_computation | async-start | bytes 2097152 | tf_op jit(solution)/shard_map/all_to_all | solution.py:403
  9.1 0.9 copy-start.5
  24.8 85.0 %copy-start.1 = (s32[8]{0:T(128)S(1)}, s32[8]{0:T(128)}, u32[]{:S(2)}) copy-start(s32[8]{0:T(128)} %live.3) | copy-start | bytes 100
  109.8 3.4 %copy-start = (bf16[64,128,512]{2,1,0:T(8,128)(2,1)S(1)}, bf16[64,128,512]{2,1,0:T(8,128)(2,1)}, u32[]{:S(2)}) copy-start(bf16[64,128,512]{2,1,0:T(8,128)(2,1)} %get-tuple-element.16.kv_ref) | copy-start | bytes 25165828
  271.7 18.0 %all-to-all-start.1 = ((bf16[4,2,256,256]{3,2,1,0:T(8,128)(2,1)}), bf16[4,2,256,256]{3,2,1,0:T(8,128)(2,1)S(1)}, u32[]{:S(2)}, u32[]{:S(2)}) async-start(bf16[4,2,256,256]{3,2,1,0:T(8,128)(2,1)} %pad_maximum_fusion.4), calls=%async_computation.1 | async-start | bytes 2097152 | tf_op jit(solution)/shard_map/all_to_all | solution.py:403

commit v4 on v3

--- a/solution.py
+++ b/solution.py
@@ -204,15 +204,15 @@
     pl.semaphore_wait(barrier, len(devices))
 
 
-def exchange(heads, sent_ref, got_ref, own_sem, send_sem, recv_sem):
+def exchange(heads, sent_ref, landing, own_sem, send_sem, recv_sem):
     me = lax.axis_index("head")
-    started = [pltpu.make_async_copy(sent_ref.at[me], got_ref.at[me], own_sem)]
+    started = [pltpu.make_async_copy(sent_ref.at[me], landing, own_sem)]
     for k in range(1, heads):
         peer = (me + k) % heads
         started.append(
             pltpu.make_async_remote_copy(
                 src_ref=sent_ref.at[peer],
-                dst_ref=got_ref.at[me],
+                dst_ref=landing,
                 send_sem=send_sem.at[k - 1],
                 recv_sem=recv_sem.at[k - 1],
                 device_id={"head": peer},
@@ -230,15 +230,18 @@
 
 
 def gather_kernel(
-    n, heads, mine_ref, sent_ref, all_ref, got_ref, own_sem, send_sem, recv_sem, *head_sems
+    n, heads, mine_ref, sent_ref, all_ref, got_ref, send_sem, recv_sem, *sems
 ):
     place, index_of = ring_place(n)
     beside = (index_of(place + 1), index_of(place - 1))
     meet(beside, heads)
-    own = pltpu.make_async_copy(
-        mine_ref, all_ref.at[pl.ds(index_of(place) * QB_DEV, QB_DEV)], own_sem
-    )
-    own.start()
+    first_sems, head_sems = sems[:3], sems[3:]
+    share = QB_DEV // heads
+    landing = all_ref.at[
+        pl.ds(lax.axis_index("blk") * QB_DEV + lax.axis_index("head") * share, share)
+    ]
+    for copy in exchange(heads, mine_ref, landing, *first_sems):
+        copy.wait()
     size = QB_DEV // 4
 
     def copy_of(step, way, part):
@@ -246,7 +249,7 @@
         first = (way * 2 + part) * size
         there = all_ref.at[pl.ds(origin * QB_DEV + first, size)]
         return pltpu.make_async_remote_copy(
-            src_ref=mine_ref.at[pl.ds(first, size)] if step == 0 else there,
+            src_ref=there,
             dst_ref=there,
             send_sem=send_sem.at[way, part, step],
             recv_sem=recv_sem.at[way, part, step],
@@ -258,7 +261,7 @@
     copies = {}
     for step in range(n):
         if step == 1:
-            swaps = exchange(heads, sent_ref, got_ref, *head_sems)
+            swaps = exchange(heads, sent_ref, got_ref.at[lax.axis_index("head")], *head_sems)
         for part in range(2):
             for way in range(2):
                 if step > 0:
@@ -268,7 +271,6 @@
                     copies[step, way, part].start()
     for copy in copies.values():
         copy.wait_send()
-    own.wait()
     for copy in swaps:
         copy.wait()
 
@@ -278,12 +280,13 @@
     return pl.pallas_call(
         functools.partial(gather_kernel, n, sent.shape[0]),
         out_shape=[
-            jax.ShapeDtypeStruct((n * mine.shape[0],) + mine.shape[1:], mine.dtype),
+            jax.ShapeDtypeStruct((n * QB_DEV,) + mine.shape[2:], mine.dtype),
             jax.ShapeDtypeStruct(sent.shape, sent.dtype),
         ],
         in_specs=[pl.BlockSpec(memory_space=pl.ANY)] * 2,
         out_specs=[pl.BlockSpec(memory_space=pl.ANY)] * 2,
-        scratch_shapes=[pltpu.SemaphoreType.DMA, steps, steps]
+        scratch_shapes=[steps, steps]
+        + exchange_semaphores(sent.shape[0])
         + exchange_semaphores(sent.shape[0]),
         compiler_params=pltpu.CompilerParams(collective_id=0, has_side_effects=True),
     )(mine, sent)
@@ -313,7 +316,7 @@
     fetches = {}
     for step in range(n):
         if step == 1:
-            swaps = exchange(heads, sent_ref, got_ref, *head_sems)
+            swaps = exchange(heads, sent_ref, got_ref.at[lax.axis_index("head")], *head_sems)
         for way, pair in lanes:
             if step > 0:
                 copies[step - 1, way, pair].wait_recv()
@@ -408,7 +411,6 @@
     def as_rows(got):
         return [got[:, n].transpose(1, 0, 2).reshape(share_rows, -1) for n in range(got.shape[1])]
 
-    key_local, value_local = as_blocks(swapped(for_heads([key_rows, value_rows])))
     mine = lax.axis_index("blk") * QB_DEV + jnp.arange(QB_DEV, dtype=jnp.int32)[:, None]
     slots = jnp.concatenate(
         [mine, (mine + local_offset + blocks) % blocks, expander_device * QB_DEV + expander_block],
@@ -417,11 +419,12 @@
     row = jnp.arange(BS, dtype=jnp.int32) * BS
     words = (drop_seed * 40503)[..., None] + row
 
-    mixed = []
-    for pair in range(pairs):
-        columns = slice(pair * PAIR, (pair + 1) * PAIR)
-        mixed += [key_local[:, columns], value_local[:, columns]]
-    mixed = jnp.concatenate(mixed, axis=1).reshape(QB_DEV, BS, pairs * 2 * PAIR)
+    mixed = jnp.stack(
+        [m.reshape(share_rows, head_count, pairs, PAIR) for m in (key_rows, value_rows)], axis=3
+    )
+    mixed = mixed.transpose(1, 0, 2, 3, 4).reshape(
+        head_count, share_rows // BS, BS, pairs * 2 * PAIR
+    )
     kv, got = gather_blocks(mixed, for_heads([query_rows, out_grad]), peer_count)
     query_local, grad_local = as_blocks(got)
     parts, terms = [], []

time: 293 us -> 296 us (1.010)
  Pallas kernels: 241 us -> 255 us
  waiting for transfers between devices: 23.8 us -> 11.9 us
  starting transfers between devices: 7.85 us -> 3.51 us
  local copies, waits for them, and re-layouts: 14.8 us -> 18.3 us
    pallas_call x1, Pallas kernels: 83.7 us -> 97.3 us  [gather_blocks(): pl.pallas_call(functools.partial(gather_kernel, n, sent.shape[0]), out_sh...]
    all_to_all x2 -> x1, waiting for transfers between devices: 23.8 us -> 11.9 us  [swapped(): return lax.all_to_all(sent, 'head', split_axis=0, concat_axis=0, tiled=True)]
    all_to_all x2 -> x1, starting transfers between devices: 7.85 us -> 3.51 us  [swapped(): return lax.all_to_all(sent, 'head', split_axis=0, concat_axis=0, tiled=True)]
    unnamed x28 -> x20, local copies, waits for them, and re-layouts: 10.9 us -> 10.8 us
  transfers between devices with their start and end apart: 2 -> 1, of which waited for: 2 -> 1; matrix products, arithmetic and copies ran while one was open for 2% -> 1% of each run, Pallas kernels for 0% -> 0%
where the time goes in v4:
time: 296 us
  Pallas kernels  255 us (86%)
  local copies, waits for them, and re-layouts  18.3 us (6%)
  waiting for transfers between devices  11.9 us (4%)
  other arithmetic  6.15 us (2%)
  starting transfers between devices  3.51 us (1%)
    pallas_call x1, Pallas kernels, gather_blocks(): pl.pallas_call(functools.partial(gather_kernel, n, sent.shape[0]), out_sh...  97.3 us
    pallas_call x1, Pallas kernels, reduce_blocks(): pl.pallas_call(functools.partial(reduce_kernel, n, pairs, sent.shape[0]),...  83.5 us
    pallas_call x2, Pallas kernels, attend(): pl.pallas_call(attention_kernel, grid_spec=pltpu.PrefetchScalarGridSpec(n...  74 us
    all_to_all x1, waiting for transfers between devices, swapped(): return lax.all_to_all(sent, 'head', split_axis=0, concat_axis=0, tiled=True)  11.9 us
    unnamed x20, local copies, waits for them, and re-layouts  10.8 us
  transfers between devices with their start and end apart: 1, of which 1 were waited for; matrix products, arithmetic and copies ran while one was open for 1% of the time, Pallas kernels for 0%

profile of v4, /device:TPU:0, one launch (start us, length us, event | category | flops | bytes accessed | tf_op | source)
XLA Modules:
  0.0 295.7 jit_solution(14671287834988984058)
XLA Ops:
  0.7 0.8 copy.45
  1.5 0.8 copy.46
  2.2 0.7 broadcast_multiply_fusion
  3.1 1.2 copy.49
  4.6 1.4 stack_reshape.18
  6.0 1.1 copy.47
  7.1 0.4 stack_reshape.19
  7.5 1.1 copy.48
  8.6 2.6 maximum_bitcast_fusion
  11.2 1.3 reshape.49.mine_ref
  12.9 1.1 pad_maximum_fusion.sent_ref
  14.0 97.3 %shard_map.120 = (bf16[64,128,512]{2,1,0:T(8,128)(2,1)}, bf16[4,2,256,256]{3,2,1,0:T(8,128)(2,1)}) custom-call(bf16[4,2,128,512]{3,2,1,0:T(8,128)(2,1)} %reshape.49.mine_ref, bf16[4,2,256,256]{3,2,1,0:T(8,128)(2,1)} %pad_maximum_fusion.sent_ref), custom_call_target="tpu_custom_call" | custom-call | tf_op jit(solution)/shard_map/pallas_call | solution.py:280
  111.3 1.3 fusion.2
  112.8 3.4 %copy-done = bf16[64,128,512]{2,1,0:T(8,128)(2,1)S(1)} copy-done((bf16[64,128,512]{2,1,0:T(8,128)(2,1)S(1)}, bf16[64,128,512]{2,1,0:T(8,128)(2,1)}, u32[]{:S(2)}) %copy-start) | copy-done | bytes 8388632
  116.1 36.9 %shard_map.122 = (bf16[1024,128]{1,0:T(8,128)(2,1)S(1)}, bf16[1024,128]{1,0:T(8,128)(2,1)S(1)}, bf16[64,128,256]{2,1,0:T(8,128)(2,1)S(1)}) custom-call(s32[8,16]{1,0:T(8,128)S(1)} %pad_add_fusion.2.slots, s32[8]{0:T(128)S(1)} %copy-done.1, bf16[1024,256]{1,0:T(8,128)(2,1)S(1)} %bitcast.50, bf16[1024,256]{1,0:T(8,128)(2,1)S(1)} %bitcast.48, ...), custom_call_target="tpu_custom_call" | custom-call | flops 4898947072 | bytes 16777216 | tf_op jit(solution)/shard_map/pallas_call | solution.py:140
  153.0 37.1 %shard_map.121 = (bf16[1024,128]{1,0:T(8,128)(2,1)S(1)}, bf16[1024,128]{1,0:T(8,128)(2,1)S(1)}, bf16[64,128,256]{2,1,0:T(8,128)(2,1)S(1)}) custom-call(s32[8,16]{1,0:T(8,128)S(1)} %pad_add_fusion.2.slots, s32[8]{0:T(128)S(1)} %copy-done.1, bf16[1024,256]{1,0:T(8,128)(2,1)S(1)} %bitcast.51, bf16[1024,256]{1,0:T(8,128)(2,1)S(1)} %bitcast.49, ...), custom_call_target="tpu_custom_call" | custom-call | flops 4898947072 | bytes 16777216 | tf_op jit(solution)/shard_map/pallas_call | solution.py:140
  190.4 83.5 %shard_map.123 = (bf16[4,2,256,256]{3,2,1,0:T(8,128)(2,1)S(1)}, bf16[8,128,256]{2,1,0:T(8,128)(2,1)S(1)}, bf16[8,128,256]{2,1,0:T(8,128)(2,1)S(1)}) custom-call(bf16[4,2,256,256]{3,2,1,0:T(8,128)(2,1)S(1)} %pad_maximum_fusion.1.sent_ref, bf16[64,128,256]{2,1,0:T(8,128)(2,1)S(1)} %get-tuple-element.21.refs_0_, bf16[64,128,256]{2,1,0:T(8,128)(2,1)S(1)} %get-tuple-element.22.refs_1_), custom_call_target="tpu_custom_call" | custom-call | tf_op jit(solution)/shard_map/pallas_call | solution.py:356
  274.1 1.1 pad_maximum_fusion.2
  275.2 3.5 %all-to-all-start = ((bf16[4,2,256,256]{3,2,1,0:T(8,128)(2,1)}), bf16[4,2,256,256]{3,2,1,0:T(8,128)(2,1)S(1)}, u32[]{:S(2)}, u32[]{:S(2)}) async-start(bf16[4,2,256,256]{3,2,1,0:T(8,128)(2,1)} %pad_maximum_fusion.2), calls=%async_computation | async-start | bytes 2097152 | tf_op jit(solution)/shard_map/all_to_all | solution.py:406
  279.0 1.0 copy.58
  280.2 1.0 copy.57
  281.2 11.9 %all-to-all-done = bf16[4,2,256,256]{3,2,1,0:T(8,128)(2,1)S(1)} async-done(((bf16[4,2,256,256]{3,2,1,0:T(8,128)(2,1)}), bf16[4,2,256,256]{3,2,1,0:T(8,128)(2,1)S(1)}, u32[]{:S(2)}, u32[]{:S(2)}) %all-to-all-start) | async-done | bytes 1048608 | tf_op jit(solution)/shard_map/all_to_all | solution.py:406
  293.4 1.0 copy.60
  294.7 1.0 copy.59
  (34 shorter events, 2.3 us)
Async XLA Ops:
  0.6 6.5 %copy-start.2 = (bf16[256,1024]{1,0:T(8,128)(2,1)S(1)}, bf16[256,1024]{1,0:T(8,128)(2,1)}, u32[]{:S(2)}) copy-start(bf16[256,1024]{1,0:T(8,128)(2,1)} %param.11) | copy-start | bytes 1572868
  7.1 5.4 %copy-start.3 = (bf16[256,1024]{1,0:T(8,128)(2,1)S(1)}, bf16[256,1024]{1,0:T(8,128)(2,1)}, u32[]{:S(2)}) copy-start(bf16[256,1024]{1,0:T(8,128)(2,1)} %param.12) | copy-start | bytes 1572868
  12.5 100.1 %copy-start.4 = (s32[8,11]{1,0:T(8,128)S(1)}, s32[8,11]{1,0:T(8,128)}, u32[]{:S(2)}) copy-start(s32[8,11]{1,0:T(8,128)} %param.15) | copy-start | bytes 1060
  12.7 100.1 %copy-start.1 = (s32[8]{0:T(128)S(1)}, s32[8]{0:T(128)}, u32[]{:S(2)}) copy-start(s32[8]{0:T(128)} %live.3) | copy-start | bytes 100
  112.7 3.4 %copy-start = (bf16[64,128,512]{2,1,0:T(8,128)(2,1)S(1)}, bf16[64,128,512]{2,1,0:T(8,128)(2,1)}, u32[]{:S(2)}) copy-start(bf16[64,128,512]{2,1,0:T(8,128)(2,1)} %get-tuple-element.16.kv_ref) | copy-start | bytes 25165828
  275.2 18.0 %all-to-all-start = ((bf16[4,2,256,256]{3,2,1,0:T(8,128)(2,1)}), bf16[4,2,256,256]{3,2,1,0:T(8,128)(2,1)S(1)}, u32[]{:S(2)}, u32[]{:S(2)}) async-start(bf16[4,2,256,256]{3,2,1,0:T(8,128)(2,1)} %pad_maximum_fusion.2), calls=%async_computation | async-start | bytes 2097152 | tf_op jit(solution)/shard_map/all_to_all | solution.py:406
